TPU v7x, 256 devices: a whole 4x4x8 slice. The times are simulated.
256 devices in a mesh: fsdp: 8 (over y, z_hi), replica: 32 (over x, z_lo, core).
Axes of the slice: x: 4, y: 4, z: 8 (z_hi: 2, z_lo: 4; z = z_hi * 4 + z_lo), core: 2. Of those that a mesh axis runs over, the one named last changes fastest.
Arguments:
- params: bfloat16 [32, 8, 2048, 512], P('replica', None, 'fsdp'), may hold values from -2.390625 to 2.390625
- momentum: bfloat16 [32, 8, 2048, 512], P('replica', None, 'fsdp'), may hold values from -6 to 6
- grads: bfloat16 [2, 32, 8, 2048, 512], P(None, 'replica', None, 'fsdp'), may hold values from -6 to 6
Outputs:
- new_params: bfloat16 [32, 8, 2048, 512], P('replica', None, 'fsdp')
- new_momentum: bfloat16 [32, 8, 2048, 512], P('replica', None, 'fsdp')
All inputs are finite; a program needn't handle non-finite values.
Results may differ from a plain program's by a relative error of at most 0.013.
Values may be sent and summed in bfloat16 or wider, within the bound.
No kernel may reach another device: no remote copies, remote signals or barrier semaphores. Data moves between devices by JAX's collectives and lax.ppermute only.
A program may use at most 128 MiB of HBM per device.

v0:
```python
import math

import jax
import jax.numpy as jnp
from jax import lax
from jax.sharding import PartitionSpec as P

ROWS = 2048
COLS = 512
NS_ITERS = 3
STEPS = 2


BETA = 0.95
LEARN = 0.5
COEF_A = 3.4445
COEF_B = -4.775
COEF_C = 2.0315


def partner(value, axis, apart):
    mask = 2**apart
    pairs = [(source, source ^ mask) for source in range(lax.axis_size(axis))]
    return lax.ppermute(value, axis, pairs)


def newton_schulz(matrix):
    xf = matrix.astype(jnp.float32)
    total = jnp.sqrt(jnp.sum(xf * xf))
    ycur = (xf / (total + 1e-07)).astype(jnp.bfloat16)
    for _ in range(NS_ITERS):
        gram = lax.dot_general(
            ycur, ycur, (((0,), (0,)), ((), ())), preferred_element_type=jnp.float32
        ).astype(jnp.bfloat16)
        square = jnp.dot(gram, gram, preferred_element_type=jnp.float32)
        poly = (COEF_B * gram.astype(jnp.float32) + COEF_C * square).astype(jnp.bfloat16)
        ycur = (
            COEF_A * ycur.astype(jnp.float32)
            + jnp.dot(ycur, poly, preferred_element_type=jnp.float32)
        ).astype(jnp.bfloat16)
    return ycur


def orthogonalize(owned):
    return lax.map(newton_schulz, owned[0])[None]


def shards(params, momentum, grads):
    owners = lax.axis_size("fsdp")
    mats = params.shape[1]
    row_part = params.shape[2]
    cols = params.shape[3]
    per_owner = mats // owners
    step_scale = LEARN * 0.2 * math.sqrt(max(ROWS, COLS))
    pcur = params[0]
    mcur = momentum[0]
    for step in range(STEPS):
        grad = grads[step, 0].astype(jnp.float32)
        m_new = (BETA * mcur.astype(jnp.float32) + grad).astype(jnp.bfloat16)
        nest = (grad + BETA * m_new.astype(jnp.float32)).astype(jnp.bfloat16)
        grouped = nest.reshape(owners, per_owner, row_part, cols)
        owned = orthogonalize(
            lax.all_to_all(grouped, "fsdp", split_axis=0, concat_axis=2, tiled=True)
        )
        returned = lax.all_to_all(owned, "fsdp", split_axis=2, concat_axis=0, tiled=True)
        update = returned.reshape(mats, row_part, cols)
        local = (pcur.astype(jnp.float32) - step_scale * update.astype(jnp.float32)).astype(
            jnp.bfloat16
        )
        l_peer, m_peer = partner((local, m_new), "replica", step)
        pcur = (0.5 * (local.astype(jnp.float32) + l_peer.astype(jnp.float32))).astype(jnp.bfloat16)
        mcur = (0.5 * (m_new.astype(jnp.float32) + m_peer.astype(jnp.float32))).astype(jnp.bfloat16)
    return (pcur[None], mcur[None])


def solution(mesh):
    return jax.shard_map(
        shards,
        mesh=mesh,
        in_specs=(
            P("replica", None, "fsdp", None),
            P("replica", None, "fsdp", None),
            P(None, "replica", None, "fsdp", None),
        ),
        out_specs=(P("replica", None, "fsdp", None), P("replica", None, "fsdp", None)),
        check_vma=False,
    )
```

profile of v0, /device:TPU:66, one launch (start us, length us, event | category | flops | bytes accessed | tf_op | source)
XLA Modules:
  0.0 332.4 jit_solution(2515015249904873186)
XLA Ops:
  0.6 4.5 %fusion.9 = bf16[8,1,256,512]{3,2,1,0:T(8,128)(2,1)} fusion(bf16[1,8,256,512]{3,2,1,0:T(8,128)(2,1)} %param.4, bf16[2,1,8,256,512]{4,3,2,1,0:T(8,128)(2,1)} %param.5), kind=kLoop, calls=%fused_computation.19 | loop fusion | flops 9437184 | bytes 6291456 | tf_op jit(solution)/shard_map/convert_element_type | solution.py:60
  5.1 9.3 %all-to-all-start = ((bf16[8,1,256,512]{3,2,1,0:T(8,128)(2,1)}), bf16[8,1,256,512]{3,2,1,0:T(8,128)(2,1)S(1)}, u32[]{:S(2)}, u32[]{:S(2)}) async-start(bf16[8,1,256,512]{3,2,1,0:T(8,128)(2,1)} %fusion.9), calls=%async_computation | async-start | bytes 4194304 | tf_op jit(solution)/shard_map/all_to_all | solution.py:63
  14.4 3.1 fusion.11
  17.6 4.1 %collective-permute-done.1 = bf16[8,256,512]{2,1,0:T(8,128)(2,1)S(1)} collective-permute-done((bf16[8,256,512]{2,1,0:T(8,128)(2,1)S(1)}, bf16[8,256,512]{2,1,0:T(8,128)(2,1)S(1)}, u32[]{:S(2)}, u32[]{:S(2)}) %collective-permute-start.1) | collective-permute-done | bytes 2097184 | tf_op jit(solution)/shard_map/ppermute | solution.py:24
  21.7 3.5 %fusion.18 = (bf16[8,1,256,512]{3,2,1,0:T(8,128)(2,1)}, bf16[8,256,512]{2,1,0:T(8,128)(2,1)}) fusion(bf16[2,1,8,256,512]{4,3,2,1,0:T(8,128)(2,1)S(1)} %copy-done.1, bf16[8,256,512]{2,1,0:T(8,128)(2,1)S(1)} %collective-permute-done.1, bf16[8,256,512]{2,1,0:T(8,128)(2,1)S(1)} %fusion.11), kind=kLoop, calls=%fused_computation.42 | loop fusion | flops 14680064 | bytes 10485760 | tf_op jit(solution)/shard_map/reshape | solution.py:61
  25.2 42.6 %all-to-all-done = bf16[8,1,256,512]{3,2,1,0:T(8,128)(2,1)S(1)} async-done(((bf16[8,1,256,512]{3,2,1,0:T(8,128)(2,1)}), bf16[8,1,256,512]{3,2,1,0:T(8,128)(2,1)S(1)}, u32[]{:S(2)}, u32[]{:S(2)}) %all-to-all-start) | async-done | bytes 2097184 | tf_op jit(solution)/shard_map/all_to_all | solution.py:63
  69.1 25.7 %all-to-all-start.2 = ((bf16[8,1,256,512]{3,2,1,0:T(8,128)(2,1)}), bf16[8,1,256,512]{3,2,1,0:T(8,128)(2,1)S(1)}, u32[]{:S(2)}, u32[]{:S(2)}) async-start(bf16[8,1,256,512]{3,2,1,0:T(8,128)(2,1)} %get-tuple-element.14), calls=%async_computation.2 | async-start | bytes 4194304 | tf_op jit(solution)/shard_map/all_to_all | solution.py:63
  94.9 3.3 %fusion.2 = f32[]{:T(128)} fusion(bf16[8,1,256,512]{3,2,1,0:T(8,128)(2,1)} %copy-done), kind=kLoop, calls=%fused_computation.12 | loop fusion | flops 3145727 | bytes 2097156 | tf_op jit(solution)/shard_map/while/body/eval_jaxpr/reduce_sum | solution.py:29
  103.5 5.2 %add_convert_fusion.5 = bf16[2048,512]{1,0:T(8,128)(2,1)} fusion(bf16[2048,512]{1,0:T(8,128)(2,1)} %bitcast.118, bf16[512,512]{1,0:T(8,128)(2,1)S(1)} %fusion.45), kind=kOutput, calls=%fused_computation.37 | convolution fusion | flops 1347682304 | bytes 4718592 | tf_op jit(solution)/shard_map/while/body/eval_jaxpr/dot_general | solution.py:39
  108.7 3.5 %convolution_convert_fusion.3 = bf16[512,512]{1,0:T(8,128)(2,1)S(1)} fusion(bf16[2048,512]{1,0:T(8,128)(2,1)} %add_convert_fusion.5), kind=kOutput, calls=%fused_computation.73 | convolution fusion | flops 1074003968 | bytes 2621440 | tf_op jit(solution)/shard_map/while/body/eval_jaxpr/dot_general | solution.py:32
  112.2 5.1 %add_convert_fusion.4 = bf16[2048,512]{1,0:T(8,128)(2,1)} fusion(bf16[2048,512]{1,0:T(8,128)(2,1)} %add_convert_fusion.5, bf16[512,512]{1,0:T(8,128)(2,1)S(1)} %convolution_convert_fusion.3), kind=kOutput, calls=%fused_computation.36 | convolution fusion | flops 1347682304 | bytes 4718592 | tf_op jit(solution)/shard_map/while/body/eval_jaxpr/dot_general | solution.py:39
  117.3 3.5 %convolution_convert_fusion.2 = bf16[512,512]{1,0:T(8,128)(2,1)S(1)} fusion(bf16[2048,512]{1,0:T(8,128)(2,1)} %add_convert_fusion.4), kind=kOutput, calls=%fused_computation.72 | convolution fusion | flops 1074003968 | bytes 2621440 | tf_op jit(solution)/shard_map/while/body/eval_jaxpr/dot_general | solution.py:32
  120.8 5.2 %fusion.15 = bf16[1,1,2048,512]{3,2,1,0:T(8,128)(2,1)} fusion(bf16[2048,512]{1,0:T(8,128)(2,1)} %add_convert_fusion.4, bf16[512,512]{1,0:T(8,128)(2,1)S(1)} %convolution_convert_fusion.2), kind=kOutput, calls=%fused_computation.39 | convolution fusion | flops 1347682304 | bytes 4718592 | tf_op jit(solution)/shard_map/while/body/eval_jaxpr/dot_general | solution.py:39
  126.0 7.5 %copy.22 = bf16[1,1,2048,512]{3,1,0,2:T(2,128)(2,1)} copy(bf16[1,1,2048,512]{3,2,1,0:T(8,128)(2,1)} %fusion.15) | data formatting | bytes 4194304 | tf_op jit(solution)/shard_map/broadcast_in_dim | solution.py:45
  134.0 15.4 %reduce.5 = bf16[2048,512]{1,0:T(8,128)(2,1)} reduce(bf16[2048,1,1,512]{3,2,1,0:T(2,128)(2,1)} %bitcast.114, bf16[]{:T(256)} %broadcast.146), dimensions={1,2}, to_apply=%bitcast.113.reduce_sub_computation | reduce | bytes 4194306
  149.4 6.3 %reshape.136 = bf16[8,2,65536]{2,1,0:T(2,128)(2,1)} reshape(bf16[2048,512]{1,0:T(8,128)(2,1)} %reduce.5) | data formatting | bytes 4194304
  155.7 9.6 %all-to-all-start.1 = ((bf16[8,2,65536]{2,1,0:T(2,128)(2,1)}), bf16[8,2,65536]{2,1,0:T(2,128)(2,1)}, u32[]{:S(2)}, u32[]{:S(2)}) async-start(bf16[8,2,65536]{2,1,0:T(2,128)(2,1)} %reshape.136), calls=%async_computation.1 | async-start | bytes 4194304 | tf_op jit(solution)/shard_map/all_to_all | solution.py:65
  169.4 3.8 %add_convert_fusion.2 = bf16[2048,512]{1,0:T(8,128)(2,1)S(1)} fusion(bf16[2048,512]{1,0:T(8,128)(2,1)} %bitcast.119, bf16[512,512]{1,0:T(8,128)(2,1)S(1)} %fusion.42), kind=kOutput, calls=%fused_computation.31 | convolution fusion | flops 1347682304 | bytes 4718592 | tf_op jit(solution)/shard_map/while/body/eval_jaxpr/dot_general | solution.py:39
  174.6 2.9 add_convert_fusion.1
  177.5 3.6 %convolution_convert_fusion = bf16[512,512]{1,0:T(8,128)(2,1)S(1)} fusion(bf16[2048,512]{1,0:T(8,128)(2,1)} %add_convert_fusion.1), kind=kOutput, calls=%fused_computation.70 | convolution fusion | flops 1074003968 | bytes 2621440 | tf_op jit(solution)/shard_map/while/body/eval_jaxpr/dot_general | solution.py:32
  184.1 7.5 %copy.21 = bf16[1,1,2048,512]{3,1,0,2:T(2,128)(2,1)} copy(bf16[1,1,2048,512]{3,2,1,0:T(8,128)(2,1)} %fusion.16) | data formatting | bytes 4194304 | tf_op jit(solution)/shard_map/broadcast_in_dim | solution.py:45
  191.5 14.1 %reduce.4 = bf16[2048,512]{1,0:T(8,128)(2,1)S(1)} reduce(bf16[2048,1,1,512]{3,2,1,0:T(2,128)(2,1)} %bitcast.115, bf16[]{:T(256)} %broadcast.146), dimensions={1,2}, to_apply=%bitcast.112.reduce_sub_computation | reduce | bytes 4194306
  205.6 3.8 %reshape.134 = bf16[8,2,65536]{2,1,0:T(2,128)(2,1)} reshape(bf16[2048,512]{1,0:T(8,128)(2,1)S(1)} %reduce.4) | data formatting | bytes 4194304
  209.4 9.6 %all-to-all-start.3 = ((bf16[8,2,65536]{2,1,0:T(2,128)(2,1)}), bf16[8,2,65536]{2,1,0:T(2,128)(2,1)}, u32[]{:S(2)}, u32[]{:S(2)}) async-start(bf16[8,2,65536]{2,1,0:T(2,128)(2,1)} %reshape.134), calls=%async_computation.3 | async-start | bytes 4194304 | tf_op jit(solution)/shard_map/all_to_all | solution.py:65
  219.0 6.8 %reshape.137 = bf16[2048,1,1,512]{3,2,1,0:T(2,128)(2,1)} reshape(bf16[8,2,65536]{2,1,0:T(2,128)(2,1)} %all-to-all-done.1) | data formatting | bytes 4194304
  225.8 7.9 %convert_multiply_fusion.4 = f32[1,1,2048,512]{3,1,0,2:T(1,128)S(1)} fusion(bf16[2048,1,1,512]{3,2,1,0:T(2,128)(2,1)} %reshape.137), kind=kLoop, calls=%fused_computation.34 | loop fusion | flops 2097152 | bytes 6291456 | tf_op jit(solution)/shard_map/mul | solution.py:67
  240.2 6.8 %reshape.135 = bf16[2048,1,1,512]{3,2,1,0:T(2,128)(2,1)} reshape(bf16[8,2,65536]{2,1,0:T(2,128)(2,1)} %all-to-all-done.3) | data formatting | bytes 4194304
  247.0 7.9 %convert_multiply_fusion.3 = f32[1,1,2048,512]{3,1,0,2:T(1,128)S(1)} fusion(bf16[2048,1,1,512]{3,2,1,0:T(2,128)(2,1)} %reshape.135), kind=kLoop, calls=%fused_computation.28 | loop fusion | flops 2097152 | bytes 6291456 | tf_op jit(solution)/shard_map/mul | solution.py:67
  255.4 3.2 subtract_convert_fusion
  258.7 27.3 %collective-permute-done.3 = bf16[8,256,512]{2,1,0:T(8,128)(2,1)} collective-permute-done((bf16[8,256,512]{2,1,0:T(8,128)(2,1)S(1)}, bf16[8,256,512]{2,1,0:T(8,128)(2,1)}, u32[]{:S(2)}, u32[]{:S(2)}) %collective-permute-start.3) | collective-permute-done | bytes 2097184 | tf_op jit(solution)/shard_map/ppermute | solution.py:24
  286.0 3.6 %fusion.19 = bf16[1,8,256,512]{3,2,1,0:T(8,128)(2,1)} fusion(bf16[8,256,512]{2,1,0:T(8,128)(2,1)} %collective-permute-done.3, bf16[8,256,512]{2,1,0:T(8,128)(2,1)S(1)} %copy-done.2), kind=kLoop, calls=%fused_computation.43 | loop fusion | flops 5242880 | bytes 6291456 | tf_op jit(solution)/shard_map/broadcast_in_dim | solution.py:73
  289.6 40.9 %collective-permute-done.2 = bf16[8,256,512]{2,1,0:T(8,128)(2,1)S(1)} collective-permute-done((bf16[8,256,512]{2,1,0:T(8,128)(2,1)S(1)}, bf16[8,256,512]{2,1,0:T(8,128)(2,1)S(1)}, u32[]{:S(2)}, u32[]{:S(2)}) %collective-permute-start.2) | collective-permute-done | bytes 2097184 | tf_op jit(solution)/shard_map/ppermute | solution.py:24
  (34 shorter events, 23.2 us)
Async XLA Ops:
  5.1 62.7 %all-to-all-start = ((bf16[8,1,256,512]{3,2,1,0:T(8,128)(2,1)}), bf16[8,1,256,512]{3,2,1,0:T(8,128)(2,1)S(1)}, u32[]{:S(2)}, u32[]{:S(2)}) async-start(bf16[8,1,256,512]{3,2,1,0:T(8,128)(2,1)} %fusion.9), calls=%async_computation | async-start | bytes 4194304 | tf_op jit(solution)/shard_map/all_to_all | solution.py:63
  14.4 7.3 %copy-start.1 = (bf16[2,1,8,256,512]{4,3,2,1,0:T(8,128)(2,1)S(1)}, bf16[2,1,8,256,512]{4,3,2,1,0:T(8,128)(2,1)}, u32[]{:S(2)}) copy-start(bf16[2,1,8,256,512]{4,3,2,1,0:T(8,128)(2,1)} %param.5) | copy-start | bytes 12582916
  17.5 4.2 %collective-permute-start.1 = (bf16[8,256,512]{2,1,0:T(8,128)(2,1)S(1)}, bf16[8,256,512]{2,1,0:T(8,128)(2,1)S(1)}, u32[]{:S(2)}, u32[]{:S(2)}) collective-permute-start(bf16[8,256,512]{2,1,0:T(8,128)(2,1)S(1)} %fusion.11), channel_id=1, source_target_pairs={{0,1},{1,0},{2,3},{3,2},{4,5},{5,4},{6,7},{7,6},{8,9},{9,8},{10,11... | collective-permute-start | bytes 6291464 | tf_op jit(solution)/shard_map/ppermute | solution.py:24
  67.8 1.3 copy-start
  69.1 86.5 %all-to-all-start.2 = ((bf16[8,1,256,512]{3,2,1,0:T(8,128)(2,1)}), bf16[8,1,256,512]{3,2,1,0:T(8,128)(2,1)S(1)}, u32[]{:S(2)}, u32[]{:S(2)}) async-start(bf16[8,1,256,512]{3,2,1,0:T(8,128)(2,1)} %get-tuple-element.14), calls=%async_computation.2 | async-start | bytes 4194304 | tf_op jit(solution)/shard_map/all_to_all | solution.py:63
  100.9 1.3 copy-start.4
  155.7 53.7 %all-to-all-start.1 = ((bf16[8,2,65536]{2,1,0:T(2,128)(2,1)}), bf16[8,2,65536]{2,1,0:T(2,128)(2,1)}, u32[]{:S(2)}, u32[]{:S(2)}) async-start(bf16[8,2,65536]{2,1,0:T(2,128)(2,1)} %reshape.136), calls=%async_computation.1 | async-start | bytes 4194304 | tf_op jit(solution)/shard_map/all_to_all | solution.py:65
  168.1 1.3 copy-start.5
  177.5 3.6 %copy-start.3 = (bf16[2048,512]{1,0:T(8,128)(2,1)S(1)}, bf16[2048,512]{1,0:T(8,128)(2,1)}, u32[]{:S(2)}) copy-start(bf16[2048,512]{1,0:T(8,128)(2,1)} %add_convert_fusion.1) | copy-start | bytes 6291460
  209.4 30.8 %all-to-all-start.3 = ((bf16[8,2,65536]{2,1,0:T(2,128)(2,1)}), bf16[8,2,65536]{2,1,0:T(2,128)(2,1)}, u32[]{:S(2)}, u32[]{:S(2)}) async-start(bf16[8,2,65536]{2,1,0:T(2,128)(2,1)} %reshape.134), calls=%async_computation.3 | async-start | bytes 4194304 | tf_op jit(solution)/shard_map/all_to_all | solution.py:65
  233.7 1.6 copy-start.6
  235.3 2.2 copy-start.2
  237.4 17.9 %collective-permute-start = (bf16[8,256,512]{2,1,0:T(8,128)(2,1)}, bf16[8,256,512]{2,1,0:T(8,128)(2,1)}, u32[]{:S(2)}, u32[]{:S(2)}) collective-permute-start(bf16[8,256,512]{2,1,0:T(8,128)(2,1)} %fusion.14), channel_id=1, source_target_pairs={{0,1},{1,0},{2,3},{3,2},{4,5},{5,4},{6,7},{7,6},{8,9},{9,8},{10,11... | collective-permute-start | bytes 6291464 | tf_op jit(solution)/shard_map/ppermute | solution.py:24
  237.5 48.5 %collective-permute-start.3 = (bf16[8,256,512]{2,1,0:T(8,128)(2,1)S(1)}, bf16[8,256,512]{2,1,0:T(8,128)(2,1)}, u32[]{:S(2)}, u32[]{:S(2)}) collective-permute-start(bf16[8,256,512]{2,1,0:T(8,128)(2,1)S(1)} %copy-done.2), channel_id=1, source_target_pairs={{0,2},{1,3},{2,0},{3,1},{4,6},{5,7},{6,4},{7,5},{8,10},{9,11},{10,... | collective-permute-start | bytes 6291464 | tf_op jit(solution)/shard_map/ppermute | solution.py:24
  258.6 71.8 %collective-permute-start.2 = (bf16[8,256,512]{2,1,0:T(8,128)(2,1)S(1)}, bf16[8,256,512]{2,1,0:T(8,128)(2,1)S(1)}, u32[]{:S(2)}, u32[]{:S(2)}) collective-permute-start(bf16[8,256,512]{2,1,0:T(8,128)(2,1)S(1)} %subtract_convert_fusion), channel_id=1, source_target_pairs={{0,2},{1,3},{2,0},{3,1},{4,6},{5,7},{6,4},{7,5},{8,10},{9,11},{10,... | collective-permute-start | bytes 6291464 | tf_op jit(solution)/shard_map/ppermute | solution.py:24
where the time goes:
time: 335 us; the launch traced here: 332 us
  waiting for transfers between devices  118 us (35%)
  other arithmetic  74.7 us (22%)
  starting transfers between devices  54.5 us (16%)
  local copies, waits for them, and re-layouts  43.7 us (13%)
  matrix products  39.7 us (12%)
    ppermute x4, waiting for transfers between devices, partner(): return lax.ppermute(value, axis, pairs)  72.3 us
    all_to_all x2, waiting for transfers between devices, shards(): lax.all_to_all(grouped, 'fsdp', split_axis=0, concat_axis=2, tiled=True)  42.6 us
    all_to_all x2, starting transfers between devices, shards(): lax.all_to_all(grouped, 'fsdp', split_axis=0, concat_axis=2, tiled=True)  35 us
    unnamed x2, other arithmetic  29.5 us
    unnamed x21, local copies, waits for them, and re-layouts  28.8 us
    dot_general x6, matrix products, newton_schulz(): jnp.dot(ycur, poly, preferred_element_type=jnp.float32)  25.2 us
    all_to_all x2, starting transfers between devices, shards(): lax.all_to_all(owned, 'fsdp', split_axis=2, concat_axis=0, tiled=True)  19.2 us
    mul x2, other arithmetic, shards(): step_scale * update.astype(jnp.float32)  15.8 us
  transfers between devices with their start and end apart: 8, of which 5 were waited for; matrix products, arithmetic and copies ran while one was open for 44% of the time, Pallas kernels for 0%

commit v1 on v0

v1 whole, which is shorter than its diff:
```python
import functools
import math

import jax
import jax.numpy as jnp
from jax import lax
from jax.experimental import pallas as pl
from jax.experimental.pallas import tpu as pltpu
from jax.sharding import PartitionSpec as P

ROWS = 2048
COLS = 512
HALF = COLS // 2
PART = 256
MATS = 8
NS_ITERS = 3
STEPS = 2
PACKED = COLS + 16

BETA = 0.95
LEARN = 0.5
COEF_A = 3.4445
COEF_B = -4.775
COEF_C = 2.0315
SCALE = LEARN * 0.2 * math.sqrt(max(ROWS, COLS))

F32 = jnp.float32
BF16 = jnp.bfloat16
PAIR = jax.ShapeDtypeStruct((2, PART, COLS), BF16)
WHOLE = jax.ShapeDtypeStruct((MATS, PART, COLS), BF16)
BLOCK = (1, PART, COLS)
MIB = 1 << 20


def mat_of(step, y_ref):
    return (step % 2) * 4 + (y_ref[0] + step // 2) % 4


def natural(step, y_ref):
    return (mat_of(step, y_ref), 0, 0)


def group_spec(place):
    return pl.BlockSpec(BLOCK, lambda t, y_ref: (jnp.clip(t - 2 * place, 0, 1), 0, 0))


def params_of(mib):
    return pltpu.CompilerParams(vmem_limit_bytes=mib * MIB)


def cost(flops, nbytes):
    return pl.CostEstimate(flops=flops, bytes_accessed=nbytes, transcendentals=0)


def first_kernel(y_ref, m_ref, g_ref, new_ref, *nest_refs):
    t = pl.program_id(0)
    grad = g_ref[0, 0, 0].astype(F32)
    m_new = (BETA * m_ref[0].astype(F32) + grad).astype(BF16)
    new_ref[0] = m_new
    nest = (grad + BETA * m_new.astype(F32)).astype(BF16)
    for d in range(4):
        @pl.when(t // 2 == d)
        def _():
            nest_refs[d][0] = nest


def first_step(y, momentum, grads):
    return pl.pallas_call(
        first_kernel,
        grid_spec=pltpu.PrefetchScalarGridSpec(
            num_scalar_prefetch=1,
            grid=(MATS,),
            in_specs=[
                pl.BlockSpec(BLOCK, natural),
                pl.BlockSpec((1, 1, 1, PART, COLS), lambda t, y_ref: (0, 0, mat_of(t, y_ref), 0, 0)),
            ],
            out_specs=[pl.BlockSpec(BLOCK, natural)] + [group_spec(d) for d in range(4)],
        ),
        out_shape=[WHOLE] + [PAIR] * 4,
        compiler_params=params_of(16),
        cost_estimate=cost(10 * MIB, 8 * MIB),
        name="nest_first",
    )(y, momentum, grads)


def second_kernel(y_ref, m_ref, peer_ref, g_ref, *out_refs):
    t = pl.program_id(0)
    grad = g_ref[0, 0, 0].astype(F32)
    mean = (0.5 * (m_ref[0].astype(F32) + peer_ref[0].astype(F32))).astype(BF16)
    m_new = (BETA * mean.astype(F32) + grad).astype(BF16)
    nest = (grad + BETA * m_new.astype(F32)).astype(BF16)
    for d in range(4):
        @pl.when(t // 2 == d)
        def _():
            out_refs[d][0] = m_new
            out_refs[4 + d][0] = nest


def second_step(y, m_new, m_peer, grads):
    return pl.pallas_call(
        second_kernel,
        grid_spec=pltpu.PrefetchScalarGridSpec(
            num_scalar_prefetch=1,
            grid=(MATS,),
            in_specs=[
                pl.BlockSpec(BLOCK, natural),
                pl.BlockSpec(BLOCK, natural),
                pl.BlockSpec((1, 1, 1, PART, COLS), lambda t, y_ref: (1, 0, mat_of(t, y_ref), 0, 0)),
            ],
            out_specs=[group_spec(d) for d in range(4)] * 2,
        ),
        out_shape=[PAIR] * 8,
        compiler_params=params_of(16),
        cost_estimate=cost(10 * MIB, 10 * MIB),
        name="nest_second",
    )(y, m_new, m_peer, grads)


def iota(axis, shape=(HALF, HALF)):
    return lax.broadcasted_iota(jnp.int32, shape, axis)


def gram_kernel(*refs):
    blocks, out_ref = refs[:4], refs[4]
    left = [ref[0, :, :HALF] for ref in blocks]
    right = [ref[0, :, HALF:] for ref in blocks]

    def product(lhs, rhs):
        total = None
        for one, two in zip(lhs, rhs):
            term = lax.dot_general(one, two, (((0,), (0,)), ((), ())), preferred_element_type=F32)
            total = term if total is None else total + term
        return total

    out_ref[0, :HALF] = product(left, right).astype(BF16)
    top = product(left, left)
    low = product(right, right)
    out_ref[0, HALF:COLS] = jnp.where(iota(1) >= iota(0), top, low).astype(BF16)
    diagonal = jnp.sum(jnp.where(iota(1) == iota(0), low, 0.0), axis=0, keepdims=True)
    out_ref[0, COLS:] = jnp.broadcast_to(diagonal, (PACKED - COLS, HALF)).astype(BF16)


def gram(blocks):
    return pl.pallas_call(
        gram_kernel,
        grid=(2,),
        in_specs=[pl.BlockSpec(BLOCK, lambda k: (k, 0, 0))] * 4,
        out_specs=pl.BlockSpec((1, PACKED, HALF), lambda k: (k, 0, 0)),
        out_shape=jax.ShapeDtypeStruct((2, PACKED, HALF), BF16),
        compiler_params=params_of(16),
        cost_estimate=cost(2 * 2 * 4 * PART * COLS * COLS, 3 * MIB),
        name="partial_gram",
    )(*blocks)


def dot(lhs, rhs):
    return jnp.dot(lhs, rhs, preferred_element_type=F32)


def update_kernel(last, *refs):
    own_ref, peer_ref = refs[:2]
    x_refs = refs[2:6]
    if last:
        u_refs, v_refs = refs[6:10], refs[10:14]
        out_refs = refs[14:18]
        rest = refs[18:]
    else:
        out_refs = refs[6:10]
        rest = refs[10:]
    g_ref, gb_ref, r_ref, y_ref = rest
    inverse = []
    for k in range(2):
        packed = own_ref[k].astype(F32) + peer_ref[k].astype(F32)
        cross = packed[:HALF]
        mixed = packed[HALF:COLS]
        flipped = mixed.T
        top = jnp.where(iota(1) >= iota(0), mixed, flipped)
        low = jnp.where(iota(1) < iota(0), mixed, flipped)
        low = jnp.where(iota(1) == iota(0), packed[COLS : COLS + 1], low)
        diagonal = jnp.sum(jnp.where(iota(1) == iota(0), top, 0.0), axis=0, keepdims=True)
        diagonal += packed[COLS : COLS + 1]
        trace = jnp.sum(diagonal, axis=1, keepdims=True)
        inv = 1.0 / (jnp.sqrt(trace) + 1e-07)
        inverse.append(inv)
        g_ref[k, :HALF, :HALF] = top * inv * inv
        g_ref[k, :HALF, HALF:] = cross * inv * inv
        g_ref[k, HALF:, :HALF] = cross.T * inv * inv
        g_ref[k, HALF:, HALF:] = low * inv * inv
        gb_ref[k] = g_ref[k].astype(BF16)
    for d in range(4):
        for k in range(2):
            y_ref[k, d * PART : (d + 1) * PART] = (x_refs[d][k].astype(F32) * inverse[k]).astype(BF16)
    for step in range(NS_ITERS):
        for k in range(2):
            value = COEF_B * g_ref[k] + COEF_C * dot(gb_ref[k], gb_ref[k])
            r_ref[k] = value.astype(BF16)
        if step < NS_ITERS - 1:
            for k in range(2):
                value = COEF_A * g_ref[k] + dot(gb_ref[k], r_ref[k])
                g_ref[k] = value
                gb_ref[k] = value.astype(BF16)
            for k in range(2):
                value = COEF_A * g_ref[k] + dot(gb_ref[k], r_ref[k])
                g_ref[k] = value
                gb_ref[k] = value.astype(BF16)
        for d in range(4):
            for k in range(2):
                block = y_ref[k, d * PART : (d + 1) * PART]
                value = COEF_A * block.astype(F32) + dot(block, r_ref[k])
                if step < NS_ITERS - 1:
                    y_ref[k, d * PART : (d + 1) * PART] = value.astype(BF16)
                elif last:
                    mean = 0.5 * (u_refs[d][k].astype(F32) + v_refs[d][k].astype(F32))
                    out_refs[d][k] = (value + mean).astype(BF16)
                else:
                    out_refs[d][k] = value.astype(BF16)


def update(own, peer, blocks, mine=(), theirs=()):
    last = bool(mine)
    return pl.pallas_call(
        functools.partial(update_kernel, last),
        in_specs=[pl.BlockSpec(memory_space=pltpu.VMEM)] * (6 + len(mine) + len(theirs)),
        out_specs=[pl.BlockSpec(memory_space=pltpu.VMEM)] * 4,
        out_shape=[PAIR] * 4,
        scratch_shapes=[
            pltpu.VMEM((2, COLS, COLS), F32),
            pltpu.VMEM((2, COLS, COLS), BF16),
            pltpu.VMEM((2, COLS, COLS), BF16),
            pltpu.VMEM((2, 4 * PART, COLS), BF16),
        ],
        compiler_params=params_of(32),
        cost_estimate=cost(2 * 13 * 2 * COLS**3, 8 * MIB),
        name="newton_schulz",
    )(own, peer, *blocks, *mine, *theirs)


def local_kernel(y_ref, p_ref, q_ref, w_ref, out_ref):
    mean = 0.5 * (p_ref[0].astype(F32) + q_ref[0].astype(F32))
    out_ref[0] = (mean - SCALE * w_ref[0].astype(F32)).astype(BF16)


def local(y, d, params, p_peer, w):
    spot = pl.BlockSpec(BLOCK, lambda k, y_ref: natural(2 * d + k, y_ref))
    here = pl.BlockSpec(BLOCK, lambda k, y_ref: (k, 0, 0))
    return pl.pallas_call(
        local_kernel,
        grid_spec=pltpu.PrefetchScalarGridSpec(
            num_scalar_prefetch=1, grid=(2,), in_specs=[spot, spot, here], out_specs=here
        ),
        out_shape=PAIR,
        compiler_params=params_of(8),
        cost_estimate=cost(MIB, 2 * MIB),
        name="local_params",
    )(y, params, p_peer, w)


def mean_kernel(y_ref, a_ref, b_ref, *refs):
    refs[-1][0] = (0.5 * (a_ref[0].astype(F32) + b_ref[0].astype(F32))).astype(BF16)


def mean_into(y, d, own, peer, out):
    here = pl.BlockSpec(BLOCK, lambda k, y_ref: (k, 0, 0))
    held = () if out is None else (out,)
    return pl.pallas_call(
        mean_kernel,
        grid_spec=pltpu.PrefetchScalarGridSpec(
            num_scalar_prefetch=1,
            grid=(2,),
            in_specs=[here, here] + [pl.BlockSpec(memory_space=pl.ANY)] * len(held),
            out_specs=pl.BlockSpec(BLOCK, lambda k, y_ref: natural(2 * d + k, y_ref)),
        ),
        out_shape=WHOLE,
        input_output_aliases={3: 0} if held else {},
        compiler_params=params_of(8),
        cost_estimate=cost(MIB, 2 * MIB),
        name="replica_mean",
    )(y, own, peer, *held)


def flip(value, axis, mask):
    return lax.ppermute(value, axis, [(s, s ^ mask) for s in range(lax.axis_size(axis))])


def shift(value, d):
    count = lax.axis_size("fsdp")
    return lax.ppermute(value, "fsdp", [(s, (s + 2 * d) % count) for s in range(count)])


def gather_rows(groups):
    return [groups[0]] + [shift(groups[d], d) for d in (1, 2, 3)]


def after(value, *earlier):
    return lax.optimization_barrier((value,) + earlier)[0]


def shards(params, momentum, grads):
    y = (lax.axis_index("fsdp") // 2).astype(jnp.int32).reshape(1)
    params, momentum = params[0], momentum[0]

    new0, *nest0 = first_step(y, momentum, grads)
    peer0 = flip(new0, "replica", 1)
    rows0 = gather_rows(nest0)
    second = second_step(y, new0, peer0, grads)
    new1, nest1 = second[:4], second[4:]
    rows1 = gather_rows(nest1)
    p_peer = flip(after(params, peer0), "replica", 1)
    m_peer = [None] * 4
    for d in (0, 1):
        m_peer[d] = flip(new1[d], "replica", 2)

    gram0 = gram(rows0)
    other0 = flip(gram0, "fsdp", 1)
    gram1 = gram(rows1)
    other1 = flip(gram1, "fsdp", 1)

    u_own = update(gram0, other0, rows0)
    u_peer = [flip(u, "replica", 1) for u in u_own]
    for d in (2, 3):
        m_peer[d] = flip(after(new1[d], other1), "replica", 2)

    w = update(gram1, other1, rows1, u_own, u_peer)
    p_own = [None] * 4
    a_peer = [None] * 4
    back = [w[0]] + [shift(w[d], -d) for d in (1, 2, 3)]
    for d in (0, 1, 3, 2):
        p_own[d] = local(y, d, params, p_peer, back[d])
        a_peer[d] = flip(p_own[d], "replica", 2)

    p_out, m_out = None, None
    for d in (0, 1, 2, 3):
        m_out = mean_into(y, d, new1[d], m_peer[d], m_out)
    for d in (0, 1, 3, 2):
        p_out = mean_into(y, d, p_own[d], a_peer[d], p_out)
    return (p_out[None], m_out[None])


def solution(mesh):
    return jax.shard_map(
        shards,
        mesh=mesh,
        in_specs=(
            P("replica", None, "fsdp", None),
            P("replica", None, "fsdp", None),
            P(None, "replica", None, "fsdp", None),
        ),
        out_specs=(P("replica", None, "fsdp", None), P("replica", None, "fsdp", None)),
        check_vma=False,
    )
```

time: 335 us -> 198 us (0.59)
  other arithmetic: 74.7 us -> 0 us
  local copies, waits for them, and re-layouts: 43.7 us -> 3.78 us
  matrix products: 39.7 us -> 0 us
  Pallas kernels: 0 us -> 32.5 us
  starting transfers between devices: 54.5 us -> 35.2 us
  waiting for transfers between devices: 118 us -> 125 us
    all_to_all x4 -> x0, starting transfers between devices: 54.3 us -> none  [the longest x2 35 us: shards(): lax.all_to_all(grouped, 'fsdp', split_axis=0, concat_axis=2, tiled=True)]
    ppermute x4 -> x25, waiting for transfers between devices: 72.3 us -> 125 us  [the longest x16 84.1 us: flip(): lax.ppermute(value, axis, [(s, s ^ mask) for s in range(lax.axis_size(axi...]
    all_to_all x4 -> x0, waiting for transfers between devices: 45.4 us -> none  [the longest x2 42.6 us: shards(): lax.all_to_all(grouped, 'fsdp', split_axis=0, concat_axis=2, tiled=True)]
    dot_general x12 -> x0, matrix products: 39.7 us -> none  [the longest x6 25.2 us: newton_schulz(): jnp.dot(ycur, poly, preferred_element_type=jnp.float32)]
    ppermute x4 -> x25, starting transfers between devices: 0.19 us -> 35.2 us  [the longest x16 19.7 us: flip(): lax.ppermute(value, axis, [(s, s ^ mask) for s in range(lax.axis_size(axi...]
    pallas_call x0 -> x18, Pallas kernels: none -> 32.5 us  [the longest x2 16.8 us: update(): pl.pallas_call(functools.partial(update_kernel, last), in_specs=[pl.Block...]
    unnamed x2 -> x0, other arithmetic: 29.5 us -> none
    unnamed x21 -> x8, local copies, waits for them, and re-layouts: 28.8 us -> 3.78 us
  transfers between devices with their start and end apart: 8 -> 25, of which waited for: 5 -> 14; matrix products, arithmetic and copies ran while one was open for 44% -> 0% of each run, Pallas kernels for 0% -> 15%
where the time goes in v1:
time: 198 us
  waiting for transfers between devices  125 us (63%)
  starting transfers between devices  35.2 us (18%)
  Pallas kernels  32.5 us (16%)
  local copies, waits for them, and re-layouts  3.78 us (2%)
    ppermute x16, waiting for transfers between devices, flip(): lax.ppermute(value, axis, [(s, s ^ mask) for s in range(lax.axis_size(axi...  84.1 us
    ppermute x9, waiting for transfers between devices, shift(): lax.ppermute(value, 'fsdp', [(s, (s + 2 * d) % count) for s in range(coun...  41.4 us
    ppermute x16, starting transfers between devices, flip(): lax.ppermute(value, axis, [(s, s ^ mask) for s in range(lax.axis_size(axi...  19.7 us
    pallas_call x2, Pallas kernels, update(): pl.pallas_call(functools.partial(update_kernel, last), in_specs=[pl.Block...  16.8 us
    ppermute x9, starting transfers between devices, shift(): lax.ppermute(value, 'fsdp', [(s, (s + 2 * d) % count) for s in range(coun...  15.5 us
    pallas_call x8, Pallas kernels, mean_into(): pl.pallas_call(mean_kernel, grid_spec=pltpu.PrefetchScalarGridSpec(num_sc...  7.16 us
  transfers between devices with their start and end apart: 25, of which 14 were waited for; matrix products, arithmetic and copies ran while one was open for 0% of the time, Pallas kernels for 15%

profile of v1, /device:TPU:66, one launch (start us, length us, event | category | flops | bytes accessed | tf_op | source)
XLA Modules:
  0.0 197.8 jit_solution(9351291720150264178)
XLA Ops:
  0.7 2.2 %copy-done.1 = bf16[2,1,8,256,512]{4,3,2,1,0:T(8,128)(2,1)S(1)} copy-done((bf16[2,1,8,256,512]{4,3,2,1,0:T(8,128)(2,1)S(1)}, bf16[2,1,8,256,512]{4,3,2,1,0:T(8,128)(2,1)}, u32[]{:S(2)}) %copy-start.1) | copy-done | bytes 4194328
  2.8 1.6 copy-done.3
  4.4 1.6 nest_first.1
  6.1 1.7 collective-permute-start.6
  7.8 2.9 %collective-permute-start.7 = (bf16[2,256,512]{2,1,0:T(8,128)(2,1)S(1)}, bf16[2,256,512]{2,1,0:T(8,128)(2,1)S(1)}, u32[]{:S(2)}, u32[]{:S(2)}) collective-permute-start(bf16[2,256,512]{2,1,0:T(8,128)(2,1)S(1)} %get-tuple-element.34), channel_id=1, source_target_pairs={{0,128},{32,160},{64,192},{96,224},{128,0},{160,32},{192,64},{224,... | collective-permute-start | bytes 1572872 | tf_op jit(solution)/shard_map/ppermute | solution.py:287
  10.7 1.3 collective-permute-start.8
  12.0 9.7 %collective-permute-done.6.refs_1_.refs_3_ = bf16[2,256,512]{2,1,0:T(8,128)(2,1)S(1)} collective-permute-done((bf16[2,256,512]{2,1,0:T(8,128)(2,1)S(1)}, bf16[2,256,512]{2,1,0:T(8,128)(2,1)S(1)}, u32[]{:S(2)}, u32[]{:S(2)}) %collective-permute-start.6) | collective-permute-done | bytes 524320 | tf_op jit(solution)/shard_map/ppermute | solution.py:287
  21.7 12.4 %collective-permute-done.7.refs_2_.refs_4_ = bf16[2,256,512]{2,1,0:T(8,128)(2,1)S(1)} collective-permute-done((bf16[2,256,512]{2,1,0:T(8,128)(2,1)S(1)}, bf16[2,256,512]{2,1,0:T(8,128)(2,1)S(1)}, u32[]{:S(2)}, u32[]{:S(2)}) %collective-permute-start.7) | collective-permute-done | bytes 524320 | tf_op jit(solution)/shard_map/ppermute | solution.py:287
  34.2 1.3 partial_gram.3.refs_0_
  35.4 5.5 %collective-permute-start.9 = (bf16[2,528,256]{2,1,0:T(8,128)(2,1)S(1)}, bf16[2,528,256]{2,1,0:T(8,128)(2,1)S(1)}, u32[]{:S(2)}, u32[]{:S(2)}) collective-permute-start(bf16[2,528,256]{2,1,0:T(8,128)(2,1)S(1)} %partial_gram.3.refs_0_), channel_id=1, source_target_pairs={{0,32},{32,0},{64,96},{96,64},{128,160},{160,128},{192,224},{224,1... | collective-permute-start | bytes 1622024 | tf_op jit(solution)/shard_map/ppermute | solution.py:282
  40.9 3.1 %nest_second.1 = (bf16[2,256,512]{2,1,0:T(8,128)(2,1)S(1)}, bf16[2,256,512]{2,1,0:T(8,128)(2,1)S(1)}, bf16[2,256,512]{2,1,0:T(8,128)(2,1)S(1)}, bf16[2,256,512]{...) custom-call(s32[1]{0:T(128)} %bitcast.y_ref, ...), custom_call_target="tpu_custom_call" | custom-call | flops 10485760 | bytes 10485760 | tf_op jit(solution)/shard_map/nest_second/pallas_call | solution.py:100
  44.1 1.2 collective-permute-start.2
  45.3 2.4 %collective-permute-start.3 = (bf16[2,256,512]{2,1,0:T(8,128)(2,1)S(1)}, bf16[2,256,512]{2,1,0:T(8,128)(2,1)S(1)}, u32[]{:S(2)}, u32[]{:S(2)}) collective-permute-start(bf16[2,256,512]{2,1,0:T(8,128)(2,1)S(1)} %get-tuple-element.30), channel_id=1, source_target_pairs={{0,128},{32,160},{64,192},{96,224},{128,0},{160,32},{192,64},{224,... | collective-permute-start | bytes 1572872 | tf_op jit(solution)/shard_map/ppermute | solution.py:287
  47.7 1.7 collective-permute-start.4
  49.4 15.6 %collective-permute-done.9.refs_1_ = bf16[2,528,256]{2,1,0:T(8,128)(2,1)S(1)} collective-permute-done((bf16[2,528,256]{2,1,0:T(8,128)(2,1)S(1)}, bf16[2,528,256]{2,1,0:T(8,128)(2,1)S(1)}, u32[]{:S(2)}, u32[]{:S(2)}) %collective-permute-start.9) | collective-permute-done | bytes 540704 | tf_op jit(solution)/shard_map/ppermute | solution.py:282
  65.0 8.2 %newton_schulz.2 = (bf16[2,256,512]{2,1,0:T(8,128)(2,1)S(1)}, bf16[2,256,512]{2,1,0:T(8,128)(2,1)S(1)}, bf16[2,256,512]{2,1,0:T(8,128)(2,1)S(1)}, bf16[2,256,512]{2,1,0:T(8,128)(2,1)S(1)}) custom-call(bf16[2,528,256]{2,1,0:T(8,128)(2,1)S(1)} %partial_gram.3.refs_0_, bf16[2,528,256]{2,1,0:T(8,128)(2,1)S(1)} %collective-permute-done.9.refs_1_, ...), custom_call_target="tpu_custom_call" | custom-call | flops 6979321856 | bytes 8388608 | tf_op jit(solution)/shard_map/newton_schulz/pallas_call | solution.py:221
  73.4 1.3 partial_gram.2.refs_0_
  74.6 5.2 %collective-permute-start.5 = (bf16[2,528,256]{2,1,0:T(8,128)(2,1)S(1)}, bf16[2,528,256]{2,1,0:T(8,128)(2,1)S(1)}, u32[]{:S(2)}, u32[]{:S(2)}) collective-permute-start(bf16[2,528,256]{2,1,0:T(8,128)(2,1)S(1)} %partial_gram.2.refs_0_), channel_id=1, source_target_pairs={{0,32},{32,0},{64,96},{96,64},{128,160},{160,128},{192,224},{224,1... | collective-permute-start | bytes 1622024 | tf_op jit(solution)/shard_map/ppermute | solution.py:282
  83.2 21.6 %collective-permute-done.5.refs_1_ = bf16[2,528,256]{2,1,0:T(8,128)(2,1)S(1)} collective-permute-done((bf16[2,528,256]{2,1,0:T(8,128)(2,1)S(1)}, bf16[2,528,256]{2,1,0:T(8,128)(2,1)S(1)}, u32[]{:S(2)}, u32[]{:S(2)}) %collective-permute-start.5) | collective-permute-done | bytes 540704 | tf_op jit(solution)/shard_map/ppermute | solution.py:282
  104.8 8.6 %newton_schulz.3 = (bf16[2,256,512]{2,1,0:T(8,128)(2,1)S(1)}, bf16[2,256,512]{2,1,0:T(8,128)(2,1)S(1)}, bf16[2,256,512]{2,1,0:T(8,128)(2,1)S(1)}, bf16[2,256,512]{2,1,0:T(8,128)(2,1)S(1)}) custom-call(bf16[2,528,256]{2,1,0:T(8,128)(2,1)S(1)} %partial_gram.2.refs_0_, bf16[2,528,256]{2,1,0:T(8,128)(2,1)S(1)} %collective-permute-done.5.refs_1_, ...), custom_call_target="tpu_custom_call" | custom-call | flops 6979321856 | bytes 8388608 | tf_op jit(solution)/shard_map/newton_schulz/pallas_call | solution.py:221
  113.5 2.5 %collective-permute-start.18 = (bf16[2,256,512]{2,1,0:T(8,128)(2,1)S(1)}, bf16[2,256,512]{2,1,0:T(8,128)(2,1)S(1)}, u32[]{:S(2)}, u32[]{:S(2)}) collective-permute-start(bf16[2,256,512]{2,1,0:T(8,128)(2,1)S(1)} %get-tuple-element.42), channel_id=1, source_target_pairs={{0,192},{32,224},{64,0},{96,32},{128,64},{160,96},{192,128},{224,1... | collective-permute-start | bytes 1572872 | tf_op jit(solution)/shard_map/ppermute | solution.py:287
  116.0 1.8 collective-permute-start.14
  117.8 2.1 %collective-permute-start.22 = (bf16[2,256,512]{2,1,0:T(8,128)(2,1)S(1)}, bf16[2,256,512]{2,1,0:T(8,128)(2,1)S(1)}, u32[]{:S(2)}, u32[]{:S(2)}) collective-permute-start(bf16[2,256,512]{2,1,0:T(8,128)(2,1)S(1)} %get-tuple-element.47.a_ref), channel_id=1, source_target_pairs={{0,2},{1,3},{2,0},{3,1},{4,6},{5,7},{6,4},{7,5},{8,10},{9,11},{10,... | collective-permute-start | bytes 1572872 | tf_op jit(solution)/shard_map/ppermute | solution.py:282
  120.2 18.3 %collective-permute-done.18.w_ref = bf16[2,256,512]{2,1,0:T(8,128)(2,1)S(1)} collective-permute-done((bf16[2,256,512]{2,1,0:T(8,128)(2,1)S(1)}, bf16[2,256,512]{2,1,0:T(8,128)(2,1)S(1)}, u32[]{:S(2)}, u32[]{:S(2)}) %collective-permute-start.18) | collective-permute-done | bytes 524320 | tf_op jit(solution)/shard_map/ppermute | solution.py:287
  138.9 2.1 %collective-permute-start.20 = (bf16[2,256,512]{2,1,0:T(8,128)(2,1)S(1)}, bf16[2,256,512]{2,1,0:T(8,128)(2,1)S(1)}, u32[]{:S(2)}, u32[]{:S(2)}) collective-permute-start(bf16[2,256,512]{2,1,0:T(8,128)(2,1)S(1)} %local_params.7.a_ref), channel_id=1, source_target_pairs={{0,2},{1,3},{2,0},{3,1},{4,6},{5,7},{6,4},{7,5},{8,10},{9,11},{10,... | collective-permute-start | bytes 1572872 | tf_op jit(solution)/shard_map/ppermute | solution.py:282
  141.9 1.7 collective-permute-start.19
  144.7 1.8 collective-permute-start.15
  149.2 4.2 %collective-permute-done.21.b_ref = bf16[2,256,512]{2,1,0:T(8,128)(2,1)S(1)} collective-permute-done((bf16[2,256,512]{2,1,0:T(8,128)(2,1)S(1)}, bf16[2,256,512]{2,1,0:T(8,128)(2,1)S(1)}, u32[]{:S(2)}, u32[]{:S(2)}) %collective-permute-start.21) | collective-permute-done | bytes 524320 | tf_op jit(solution)/shard_map/ppermute | solution.py:282
  154.3 10.3 %collective-permute-done.20.b_ref = bf16[2,256,512]{2,1,0:T(8,128)(2,1)S(1)} collective-permute-done((bf16[2,256,512]{2,1,0:T(8,128)(2,1)S(1)}, bf16[2,256,512]{2,1,0:T(8,128)(2,1)S(1)}, u32[]{:S(2)}, u32[]{:S(2)}) %collective-permute-start.20) | collective-permute-done | bytes 524320 | tf_op jit(solution)/shard_map/ppermute | solution.py:282
  165.5 10.3 %collective-permute-done.19.b_ref = bf16[2,256,512]{2,1,0:T(8,128)(2,1)S(1)} collective-permute-done((bf16[2,256,512]{2,1,0:T(8,128)(2,1)S(1)}, bf16[2,256,512]{2,1,0:T(8,128)(2,1)S(1)}, u32[]{:S(2)}, u32[]{:S(2)}) %collective-permute-start.19) | collective-permute-done | bytes 524320 | tf_op jit(solution)/shard_map/ppermute | solution.py:282
  176.8 10.3 %collective-permute-done.17.b_ref = bf16[2,256,512]{2,1,0:T(8,128)(2,1)S(1)} collective-permute-done((bf16[2,256,512]{2,1,0:T(8,128)(2,1)S(1)}, bf16[2,256,512]{2,1,0:T(8,128)(2,1)S(1)}, u32[]{:S(2)}, u32[]{:S(2)}) %collective-permute-start.17) | collective-permute-done | bytes 524320 | tf_op jit(solution)/shard_map/ppermute | solution.py:282
  188.0 8.9 %collective-permute-done.15.b_ref = bf16[2,256,512]{2,1,0:T(8,128)(2,1)S(1)} collective-permute-done((bf16[2,256,512]{2,1,0:T(8,128)(2,1)S(1)}, bf16[2,256,512]{2,1,0:T(8,128)(2,1)S(1)}, u32[]{:S(2)}, u32[]{:S(2)}) %collective-permute-start.15) | collective-permute-done | bytes 524320 | tf_op jit(solution)/shard_map/ppermute | solution.py:282
  (44 shorter events, 13.3 us)
Async XLA Ops:
  0.6 2.2 %copy-start.1 = (bf16[2,1,8,256,512]{4,3,2,1,0:T(8,128)(2,1)S(1)}, bf16[2,1,8,256,512]{4,3,2,1,0:T(8,128)(2,1)}, u32[]{:S(2)}) copy-start(bf16[2,1,8,256,512]{4,3,2,1,0:T(8,128)(2,1)} %g_ref.3) | copy-start | bytes 12582916
  2.8 1.6 copy-start.3
  4.4 36.5 %copy-start.2 = (bf16[2,1,8,256,512]{4,3,2,1,0:T(8,128)(2,1)S(1)}, bf16[2,1,8,256,512]{4,3,2,1,0:T(8,128)(2,1)}, u32[]{:S(2)}) copy-start(bf16[2,1,8,256,512]{4,3,2,1,0:T(8,128)(2,1)} %g_ref.3) | copy-start | bytes 12582916
  6.0 34.9 %collective-permute-start = (bf16[8,256,512]{2,1,0:T(8,128)(2,1)S(1)}, bf16[8,256,512]{2,1,0:T(8,128)(2,1)S(1)}, u32[]{:S(2)}, u32[]{:S(2)}) collective-permute-start(bf16[8,256,512]{2,1,0:T(8,128)(2,1)S(1)} %get-tuple-element.26.m_ref), channel_id=1, source_target_pairs={{0,1},{1,0},{2,3},{3,2},{4,5},{5,4},{6,7},{7,6},{8,9},{9,8},{10,11... | collective-permute-start | bytes 6291464 | tf_op jit(solution)/shard_map/ppermute | solution.py:282
  6.1 15.6 %collective-permute-start.6 = (bf16[2,256,512]{2,1,0:T(8,128)(2,1)S(1)}, bf16[2,256,512]{2,1,0:T(8,128)(2,1)S(1)}, u32[]{:S(2)}, u32[]{:S(2)}) collective-permute-start(bf16[2,256,512]{2,1,0:T(8,128)(2,1)S(1)} %get-tuple-element.33), channel_id=1, source_target_pairs={{0,64},{32,96},{64,128},{96,160},{128,192},{160,224},{192,0},{224,... | collective-permute-start | bytes 1572872 | tf_op jit(solution)/shard_map/ppermute | solution.py:287
  7.8 26.4 %collective-permute-start.7 = (bf16[2,256,512]{2,1,0:T(8,128)(2,1)S(1)}, bf16[2,256,512]{2,1,0:T(8,128)(2,1)S(1)}, u32[]{:S(2)}, u32[]{:S(2)}) collective-permute-start(bf16[2,256,512]{2,1,0:T(8,128)(2,1)S(1)} %get-tuple-element.34), channel_id=1, source_target_pairs={{0,128},{32,160},{64,192},{96,224},{128,0},{160,32},{192,64},{224,... | collective-permute-start | bytes 1572872 | tf_op jit(solution)/shard_map/ppermute | solution.py:287
  10.7 23.5 %collective-permute-start.8 = (bf16[2,256,512]{2,1,0:T(8,128)(2,1)S(1)}, bf16[2,256,512]{2,1,0:T(8,128)(2,1)S(1)}, u32[]{:S(2)}, u32[]{:S(2)}) collective-permute-start(bf16[2,256,512]{2,1,0:T(8,128)(2,1)S(1)} %get-tuple-element.35), channel_id=1, source_target_pairs={{0,192},{32,224},{64,0},{96,32},{128,64},{160,96},{192,128},{224,1... | collective-permute-start | bytes 1572872 | tf_op jit(solution)/shard_map/ppermute | solution.py:287
  35.4 29.6 %collective-permute-start.9 = (bf16[2,528,256]{2,1,0:T(8,128)(2,1)S(1)}, bf16[2,528,256]{2,1,0:T(8,128)(2,1)S(1)}, u32[]{:S(2)}, u32[]{:S(2)}) collective-permute-start(bf16[2,528,256]{2,1,0:T(8,128)(2,1)S(1)} %partial_gram.3.refs_0_), channel_id=1, source_target_pairs={{0,32},{32,0},{64,96},{96,64},{128,160},{160,128},{192,224},{224,1... | collective-permute-start | bytes 1622024 | tf_op jit(solution)/shard_map/ppermute | solution.py:282
  40.9 8.4 %copy-start = (bf16[1,8,256,512]{3,2,1,0:T(8,128)(2,1)S(1)}, bf16[1,8,256,512]{3,2,1,0:T(8,128)(2,1)}, u32[]{:S(2)}) copy-start(bf16[1,8,256,512]{3,2,1,0:T(8,128)(2,1)} %param.3) | copy-start | bytes 6291460
  44.1 29.2 %collective-permute-start.2 = (bf16[2,256,512]{2,1,0:T(8,128)(2,1)S(1)}, bf16[2,256,512]{2,1,0:T(8,128)(2,1)S(1)}, u32[]{:S(2)}, u32[]{:S(2)}) collective-permute-start(bf16[2,256,512]{2,1,0:T(8,128)(2,1)S(1)} %get-tuple-element.29), channel_id=1, source_target_pairs={{0,64},{32,96},{64,128},{96,160},{128,192},{160,224},{192,0},{224,... | collective-permute-start | bytes 1572872 | tf_op jit(solution)/shard_map/ppermute | solution.py:287
  45.3 28.0 %collective-permute-start.3 = (bf16[2,256,512]{2,1,0:T(8,128)(2,1)S(1)}, bf16[2,256,512]{2,1,0:T(8,128)(2,1)S(1)}, u32[]{:S(2)}, u32[]{:S(2)}) collective-permute-start(bf16[2,256,512]{2,1,0:T(8,128)(2,1)S(1)} %get-tuple-element.30), channel_id=1, source_target_pairs={{0,128},{32,160},{64,192},{96,224},{128,0},{160,32},{192,64},{224,... | collective-permute-start | bytes 1572872 | tf_op jit(solution)/shard_map/ppermute | solution.py:287
  47.7 25.7 %collective-permute-start.4 = (bf16[2,256,512]{2,1,0:T(8,128)(2,1)S(1)}, bf16[2,256,512]{2,1,0:T(8,128)(2,1)S(1)}, u32[]{:S(2)}, u32[]{:S(2)}) collective-permute-start(bf16[2,256,512]{2,1,0:T(8,128)(2,1)S(1)} %get-tuple-element.31), channel_id=1, source_target_pairs={{0,192},{32,224},{64,0},{96,32},{128,64},{160,96},{192,128},{224,1... | collective-permute-start | bytes 1572872 | tf_op jit(solution)/shard_map/ppermute | solution.py:287
  49.4 68.5 %collective-permute-start.1 = (bf16[8,256,512]{2,1,0:T(8,128)(2,1)S(1)}, bf16[8,256,512]{2,1,0:T(8,128)(2,1)S(1)}, u32[]{:S(2)}, u32[]{:S(2)}) collective-permute-start(bf16[8,256,512]{2,1,0:T(8,128)(2,1)S(1)} %bitcast.5), channel_id=1, source_target_pairs={{0,1},{1,0},{2,3},{3,2},{4,5},{5,4},{6,7},{7,6},{8,9},{9,8},{10,11... | collective-permute-start | bytes 6291464 | tf_op jit(solution)/shard_map/ppermute | solution.py:282
  73.2 7.1 %collective-permute-start.10 = (bf16[2,256,512]{2,1,0:T(8,128)(2,1)S(1)}, bf16[2,256,512]{2,1,0:T(8,128)(2,1)S(1)}, u32[]{:S(2)}, u32[]{:S(2)}) collective-permute-start(bf16[2,256,512]{2,1,0:T(8,128)(2,1)S(1)} %get-tuple-element.36.refs_6_), channel_id=1, source_target_pairs={{0,1},{1,0},{2,3},{3,2},{4,5},{5,4},{6,7},{7,6},{8,9},{9,8},{10,11... | collective-permute-start | bytes 1572872 | tf_op jit(solution)/shard_map/ppermute | solution.py:282
  74.6 30.2 %collective-permute-start.5 = (bf16[2,528,256]{2,1,0:T(8,128)(2,1)S(1)}, bf16[2,528,256]{2,1,0:T(8,128)(2,1)S(1)}, u32[]{:S(2)}, u32[]{:S(2)}) collective-permute-start(bf16[2,528,256]{2,1,0:T(8,128)(2,1)S(1)} %partial_gram.2.refs_0_), channel_id=1, source_target_pairs={{0,32},{32,0},{64,96},{96,64},{128,160},{160,128},{192,224},{224,1... | collective-permute-start | bytes 1622024 | tf_op jit(solution)/shard_map/ppermute | solution.py:282
  79.8 1.9 collective-permute-start.11
  80.0 2.5 %collective-permute-start.12 = (bf16[2,256,512]{2,1,0:T(8,128)(2,1)S(1)}, bf16[2,256,512]{2,1,0:T(8,128)(2,1)S(1)}, u32[]{:S(2)}, u32[]{:S(2)}) collective-permute-start(bf16[2,256,512]{2,1,0:T(8,128)(2,1)S(1)} %get-tuple-element.38.refs_8_), channel_id=1, source_target_pairs={{0,1},{1,0},{2,3},{3,2},{4,5},{5,4},{6,7},{7,6},{8,9},{9,8},{10,11... | collective-permute-start | bytes 1572872 | tf_op jit(solution)/shard_map/ppermute | solution.py:282
  80.3 2.9 %collective-permute-start.13 = (bf16[2,256,512]{2,1,0:T(8,128)(2,1)S(1)}, bf16[2,256,512]{2,1,0:T(8,128)(2,1)S(1)}, u32[]{:S(2)}, u32[]{:S(2)}) collective-permute-start(bf16[2,256,512]{2,1,0:T(8,128)(2,1)S(1)} %get-tuple-element.39.refs_9_), channel_id=1, source_target_pairs={{0,1},{1,0},{2,3},{3,2},{4,5},{5,4},{6,7},{7,6},{8,9},{9,8},{10,11... | collective-permute-start | bytes 1572872 | tf_op jit(solution)/shard_map/ppermute | solution.py:282
  81.7 34.3 %collective-permute-start.23 = (bf16[2,256,512]{2,1,0:T(8,128)(2,1)S(1)}, bf16[2,256,512]{2,1,0:T(8,128)(2,1)S(1)}, u32[]{:S(2)}, u32[]{:S(2)}) collective-permute-start(bf16[2,256,512]{2,1,0:T(8,128)(2,1)S(1)} %get-tuple-element.48.a_ref), channel_id=1, source_target_pairs={{0,2},{1,3},{2,0},{3,1},{4,6},{5,7},{6,4},{7,5},{8,10},{9,11},{10,... | collective-permute-start | bytes 1572872 | tf_op jit(solution)/shard_map/ppermute | solution.py:282
  113.5 25.1 %collective-permute-start.18 = (bf16[2,256,512]{2,1,0:T(8,128)(2,1)S(1)}, bf16[2,256,512]{2,1,0:T(8,128)(2,1)S(1)}, u32[]{:S(2)}, u32[]{:S(2)}) collective-permute-start(bf16[2,256,512]{2,1,0:T(8,128)(2,1)S(1)} %get-tuple-element.42), channel_id=1, source_target_pairs={{0,192},{32,224},{64,0},{96,32},{128,64},{160,96},{192,128},{224,1... | collective-permute-start | bytes 1572872 | tf_op jit(solution)/shard_map/ppermute | solution.py:287
  116.0 22.9 %collective-permute-start.24 = (bf16[2,256,512]{2,1,0:T(8,128)(2,1)S(1)}, bf16[2,256,512]{2,1,0:T(8,128)(2,1)S(1)}, u32[]{:S(2)}, u32[]{:S(2)}) collective-permute-start(bf16[2,256,512]{2,1,0:T(8,128)(2,1)S(1)} %get-tuple-element.49.a_ref), channel_id=1, source_target_pairs={{0,2},{1,3},{2,0},{3,1},{4,6},{5,7},{6,4},{7,5},{8,10},{9,11},{10,... | collective-permute-start | bytes 1572872 | tf_op jit(solution)/shard_map/ppermute | solution.py:282
  116.0 26.0 %collective-permute-start.16 = (bf16[2,256,512]{2,1,0:T(8,128)(2,1)S(1)}, bf16[2,256,512]{2,1,0:T(8,128)(2,1)S(1)}, u32[]{:S(2)}, u32[]{:S(2)}) collective-permute-start(bf16[2,256,512]{2,1,0:T(8,128)(2,1)S(1)} %get-tuple-element.41), channel_id=1, source_target_pairs={{0,64},{32,96},{64,128},{96,160},{128,192},{160,224},{192,0},{224,... | collective-permute-start | bytes 1572872 | tf_op jit(solution)/shard_map/ppermute | solution.py:287
  116.0 28.0 %collective-permute-start.14 = (bf16[2,256,512]{2,1,0:T(8,128)(2,1)S(1)}, bf16[2,256,512]{2,1,0:T(8,128)(2,1)S(1)}, u32[]{:S(2)}, u32[]{:S(2)}) collective-permute-start(bf16[2,256,512]{2,1,0:T(8,128)(2,1)S(1)} %get-tuple-element.40), channel_id=1, source_target_pairs={{0,128},{32,160},{64,192},{96,224},{128,0},{160,32},{192,64},{224,... | collective-permute-start | bytes 1572872 | tf_op jit(solution)/shard_map/ppermute | solution.py:287
  117.8 26.9 %collective-permute-start.22 = (bf16[2,256,512]{2,1,0:T(8,128)(2,1)S(1)}, bf16[2,256,512]{2,1,0:T(8,128)(2,1)S(1)}, u32[]{:S(2)}, u32[]{:S(2)}) collective-permute-start(bf16[2,256,512]{2,1,0:T(8,128)(2,1)S(1)} %get-tuple-element.47.a_ref), channel_id=1, source_target_pairs={{0,2},{1,3},{2,0},{3,1},{4,6},{5,7},{6,4},{7,5},{8,10},{9,11},{10,... | collective-permute-start | bytes 1572872 | tf_op jit(solution)/shard_map/ppermute | solution.py:282
  138.5 14.9 %collective-permute-start.21 = (bf16[2,256,512]{2,1,0:T(8,128)(2,1)S(1)}, bf16[2,256,512]{2,1,0:T(8,128)(2,1)S(1)}, u32[]{:S(2)}, u32[]{:S(2)}) collective-permute-start(bf16[2,256,512]{2,1,0:T(8,128)(2,1)S(1)} %get-tuple-element.45.a_ref), channel_id=1, source_target_pairs={{0,2},{1,3},{2,0},{3,1},{4,6},{5,7},{6,4},{7,5},{8,10},{9,11},{10,... | collective-permute-start | bytes 1572872 | tf_op jit(solution)/shard_map/ppermute | solution.py:282
  138.9 25.8 %collective-permute-start.20 = (bf16[2,256,512]{2,1,0:T(8,128)(2,1)S(1)}, bf16[2,256,512]{2,1,0:T(8,128)(2,1)S(1)}, u32[]{:S(2)}, u32[]{:S(2)}) collective-permute-start(bf16[2,256,512]{2,1,0:T(8,128)(2,1)S(1)} %local_params.7.a_ref), channel_id=1, source_target_pairs={{0,2},{1,3},{2,0},{3,1},{4,6},{5,7},{6,4},{7,5},{8,10},{9,11},{10,... | collective-permute-start | bytes 1572872 | tf_op jit(solution)/shard_map/ppermute | solution.py:282
  141.9 34.0 %collective-permute-start.19 = (bf16[2,256,512]{2,1,0:T(8,128)(2,1)S(1)}, bf16[2,256,512]{2,1,0:T(8,128)(2,1)S(1)}, u32[]{:S(2)}, u32[]{:S(2)}) collective-permute-start(bf16[2,256,512]{2,1,0:T(8,128)(2,1)S(1)} %local_params.6.a_ref), channel_id=1, source_target_pairs={{0,2},{1,3},{2,0},{3,1},{4,6},{5,7},{6,4},{7,5},{8,10},{9,11},{10,... | collective-permute-start | bytes 1572872 | tf_op jit(solution)/shard_map/ppermute | solution.py:282
  144.0 43.1 %collective-permute-start.17 = (bf16[2,256,512]{2,1,0:T(8,128)(2,1)S(1)}, bf16[2,256,512]{2,1,0:T(8,128)(2,1)S(1)}, u32[]{:S(2)}, u32[]{:S(2)}) collective-permute-start(bf16[2,256,512]{2,1,0:T(8,128)(2,1)S(1)} %local_params.5.a_ref), channel_id=1, source_target_pairs={{0,2},{1,3},{2,0},{3,1},{4,6},{5,7},{6,4},{7,5},{8,10},{9,11},{10,... | collective-permute-start | bytes 1572872 | tf_op jit(solution)/shard_map/ppermute | solution.py:282
  144.7 52.2 %collective-permute-start.15 = (bf16[2,256,512]{2,1,0:T(8,128)(2,1)S(1)}, bf16[2,256,512]{2,1,0:T(8,128)(2,1)S(1)}, u32[]{:S(2)}, u32[]{:S(2)}) collective-permute-start(bf16[2,256,512]{2,1,0:T(8,128)(2,1)S(1)} %local_params.4.a_ref), channel_id=1, source_target_pairs={{0,2},{1,3},{2,0},{3,1},{4,6},{5,7},{6,4},{7,5},{8,10},{9,11},{10,... | collective-permute-start | bytes 1572872 | tf_op jit(solution)/shard_map/ppermute | solution.py:282

commit v2 on v1

--- a/solution.py
+++ b/solution.py
@@ -27,6 +27,7 @@
 F32 = jnp.float32
 BF16 = jnp.bfloat16
 PAIR = jax.ShapeDtypeStruct((2, PART, COLS), BF16)
+FOUR = jax.ShapeDtypeStruct((4, PART, COLS), BF16)
 WHOLE = jax.ShapeDtypeStruct((MATS, PART, COLS), BF16)
 BLOCK = (1, PART, COLS)
 MIB = 1 << 20
@@ -41,7 +42,11 @@
 
 
 def group_spec(place):
-    return pl.BlockSpec(BLOCK, lambda t, y_ref: (jnp.clip(t - 2 * place, 0, 1), 0, 0))
+    return run_of(2 * place, 2)
+
+
+def run_of(first, count):
+    return pl.BlockSpec(BLOCK, lambda t, y_ref: (jnp.clip(t - first, 0, count - 1), 0, 0))
 
 
 def params_of(mib):
@@ -92,8 +97,8 @@
     for d in range(4):
         @pl.when(t // 2 == d)
         def _():
-            out_refs[d][0] = m_new
-            out_refs[4 + d][0] = nest
+            out_refs[max(d - 1, 0)][0] = m_new
+            out_refs[3 + d][0] = nest
 
 
 def second_step(y, m_new, m_peer, grads):
@@ -107,9 +112,9 @@
                 pl.BlockSpec(BLOCK, natural),
                 pl.BlockSpec((1, 1, 1, PART, COLS), lambda t, y_ref: (1, 0, mat_of(t, y_ref), 0, 0)),
             ],
-            out_specs=[group_spec(d) for d in range(4)] * 2,
-        ),
-        out_shape=[PAIR] * 8,
+            out_specs=[run_of(0, 4)] + [group_spec(d) for d in (2, 3, 0, 1, 2, 3)],
+        ),
+        out_shape=[FOUR] + [PAIR] * 6,
         compiler_params=params_of(16),
         cost_estimate=cost(10 * MIB, 10 * MIB),
         name="nest_second",
@@ -260,15 +265,16 @@
 
 
 def mean_into(y, d, own, peer, out):
-    here = pl.BlockSpec(BLOCK, lambda k, y_ref: (k, 0, 0))
+    count = own.shape[0]
+    here = run_of(0, count)
     held = () if out is None else (out,)
     return pl.pallas_call(
         mean_kernel,
         grid_spec=pltpu.PrefetchScalarGridSpec(
             num_scalar_prefetch=1,
-            grid=(2,),
+            grid=(count,),
             in_specs=[here, here] + [pl.BlockSpec(memory_space=pl.ANY)] * len(held),
-            out_specs=pl.BlockSpec(BLOCK, lambda k, y_ref: natural(2 * d + k, y_ref)),
+            out_specs=pl.BlockSpec(BLOCK, lambda t, y_ref: natural(2 * d + t, y_ref)),
         ),
         out_shape=WHOLE,
         input_output_aliases={3: 0} if held else {},
@@ -291,8 +297,8 @@
     return [groups[0]] + [shift(groups[d], d) for d in (1, 2, 3)]
 
 
-def after(value, *earlier):
-    return lax.optimization_barrier((value,) + earlier)[0]
+def after(values, *earlier):
+    return lax.optimization_barrier((values,) + earlier)[0]
 
 
 def shards(params, momentum, grads):
@@ -301,38 +307,42 @@
 
     new0, *nest0 = first_step(y, momentum, grads)
     peer0 = flip(new0, "replica", 1)
+    p_peer = flip(after(params, peer0), "replica", 1)
     rows0 = gather_rows(nest0)
-    second = second_step(y, new0, peer0, grads)
-    new1, nest1 = second[:4], second[4:]
-    rows1 = gather_rows(nest1)
-    p_peer = flip(after(params, peer0), "replica", 1)
-    m_peer = [None] * 4
-    for d in (0, 1):
-        m_peer[d] = flip(new1[d], "replica", 2)
-
+    ma, mb, mc, *nest1 = second_step(y, new0, peer0, grads)
+    ma_peer = flip(ma, "replica", 2)
+
+    rows0 = after(rows0, ma, p_peer)
     gram0 = gram(rows0)
     other0 = flip(gram0, "fsdp", 1)
-    gram1 = gram(rows1)
+    rows1 = gather_rows(after(nest1, gram0))
+    gram1 = gram(after(rows1, ma_peer))
     other1 = flip(gram1, "fsdp", 1)
-
-    u_own = update(gram0, other0, rows0)
+    mb_peer = flip(after(mb, gram0), "replica", 2)
+
+    u_own = update(gram0, after(other0, gram1), rows0)
     u_peer = [flip(u, "replica", 1) for u in u_own]
-    for d in (2, 3):
-        m_peer[d] = flip(after(new1[d], other1), "replica", 2)
-
-    w = update(gram1, other1, rows1, u_own, u_peer)
+
+    mc_peer = flip(after(mc, other1), "replica", 2)
+    w = update(gram1, after(other1, mb_peer), rows1, u_own, u_peer)
+    back = [w[0]] + [shift(w[d], -d) for d in (1, 2, 3)]
     p_own = [None] * 4
     a_peer = [None] * 4
-    back = [w[0]] + [shift(w[d], -d) for d in (1, 2, 3)]
+    p_own[0] = local(y, 0, params, p_peer, back[0])
+    a_peer[0] = flip(p_own[0], "replica", 2)
+    p_own[1] = local(y, 1, params, p_peer, after(back[1], p_own[0]))
+    a_peer[1] = flip(p_own[1], "replica", 2)
+    p_own[3] = local(y, 3, params, p_peer, after(back[3], p_own[1]))
+    a_peer[3] = flip(p_own[3], "replica", 2)
+    p_own[2] = local(y, 2, params, p_peer, after(back[2], p_own[3], a_peer[0], mc_peer))
+    a_peer[2] = flip(p_own[2], "replica", 2)
+
+    m_out = mean_into(y, 0, ma, ma_peer, None)
+    m_out = mean_into(y, 2, mb, mb_peer, m_out)
+    m_out = mean_into(y, 3, mc, mc_peer, m_out)
+    p_out = None
     for d in (0, 1, 3, 2):
-        p_own[d] = local(y, d, params, p_peer, back[d])
-        a_peer[d] = flip(p_own[d], "replica", 2)
-
-    p_out, m_out = None, None
-    for d in (0, 1, 2, 3):
-        m_out = mean_into(y, d, new1[d], m_peer[d], m_out)
-    for d in (0, 1, 3, 2):
-        p_out = mean_into(y, d, p_own[d], a_peer[d], p_out)
+        p_out = mean_into(y, d, p_own[d], after(a_peer[d], m_out), p_out)
     return (p_out[None], m_out[None])
 
 

time: 198 us -> 179 us (0.904)
  waiting for transfers between devices: 125 us -> 109 us
    ppermute x16 -> x15, waiting for transfers between devices: 84.1 us -> 57.1 us  [flip(): lax.ppermute(value, axis, [(s, s ^ mask) for s in range(lax.axis_size(axi...]
    ppermute x9, waiting for transfers between devices: 41.4 us -> 51.4 us  [shift(): lax.ppermute(value, 'fsdp', [(s, (s + 2 * d) % count) for s in range(coun...]
    ppermute x16 -> x15, starting transfers between devices: 19.7 us -> 19.3 us  [flip(): lax.ppermute(value, axis, [(s, s ^ mask) for s in range(lax.axis_size(axi...]
    pallas_call x8 -> x7, Pallas kernels: 7.16 us -> 7.04 us  [mean_into(): pl.pallas_call(mean_kernel, grid_spec=pltpu.PrefetchScalarGridSpec(num_sc...]
  transfers between devices with their start and end apart: 25 -> 24, of which waited for: 14 -> 13; matrix products, arithmetic and copies ran while one was open for 0% -> 0% of each run, Pallas kernels for 15% -> 11%
where the time goes in v2:
time: 179 us
  waiting for transfers between devices  109 us (61%)
  starting transfers between devices  33.8 us (19%)
  Pallas kernels  32.3 us (18%)
  local copies, waits for them, and re-layouts  3.78 us (2%)
    ppermute x15, waiting for transfers between devices, flip(): lax.ppermute(value, axis, [(s, s ^ mask) for s in range(lax.axis_size(axi...  57.1 us
    ppermute x9, waiting for transfers between devices, shift(): lax.ppermute(value, 'fsdp', [(s, (s + 2 * d) % count) for s in range(coun...  51.4 us
    ppermute x15, starting transfers between devices, flip(): lax.ppermute(value, axis, [(s, s ^ mask) for s in range(lax.axis_size(axi...  19.3 us
    pallas_call x2, Pallas kernels, update(): pl.pallas_call(functools.partial(update_kernel, last), in_specs=[pl.Block...  16.8 us
    ppermute x9, starting transfers between devices, shift(): lax.ppermute(value, 'fsdp', [(s, (s + 2 * d) % count) for s in range(coun...  14.5 us
    pallas_call x7, Pallas kernels, mean_into(): pl.pallas_call(mean_kernel, grid_spec=pltpu.PrefetchScalarGridSpec(num_sc...  7.04 us
    unnamed x8, local copies, waits for them, and re-layouts  3.78 us
  transfers between devices with their start and end apart: 24, of which 13 were waited for; matrix products, arithmetic and copies ran while one was open for 0% of the time, Pallas kernels for 11%

profile of v2, /device:TPU:66, one launch (start us, length us, event | category | flops | bytes accessed | tf_op | source)
XLA Modules:
  0.0 179.2 jit_solution(11093455734103731147)
XLA Ops:
  0.7 2.2 %copy-done.1 = bf16[2,1,8,256,512]{4,3,2,1,0:T(8,128)(2,1)S(1)} copy-done((bf16[2,1,8,256,512]{4,3,2,1,0:T(8,128)(2,1)S(1)}, bf16[2,1,8,256,512]{4,3,2,1,0:T(8,128)(2,1)}, u32[]{:S(2)}) %copy-start.1) | copy-done | bytes 4194328
  2.8 1.6 copy-done.3
  4.4 1.6 nest_first.1
  6.1 4.1 %collective-permute-done.peer_ref = bf16[8,256,512]{2,1,0:T(8,128)(2,1)S(1)} collective-permute-done((bf16[8,256,512]{2,1,0:T(8,128)(2,1)S(1)}, bf16[8,256,512]{2,1,0:T(8,128)(2,1)S(1)}, u32[]{:S(2)}, u32[]{:S(2)}) %collective-permute-start) | collective-permute-done | bytes 2097184 | tf_op jit(solution)/shard_map/ppermute | solution.py:288
  10.4 1.6 collective-permute-start.2
  12.0 2.9 %collective-permute-start.3 = (bf16[2,256,512]{2,1,0:T(8,128)(2,1)S(1)}, bf16[2,256,512]{2,1,0:T(8,128)(2,1)S(1)}, u32[]{:S(2)}, u32[]{:S(2)}) collective-permute-start(bf16[2,256,512]{2,1,0:T(8,128)(2,1)S(1)} %get-tuple-element.54), channel_id=1, source_target_pairs={{0,128},{32,160},{64,192},{96,224},{128,0},{160,32},{192,64},{224,... | collective-permute-start | bytes 1572872 | tf_op jit(solution)/shard_map/ppermute | solution.py:293
  14.9 1.3 collective-permute-start.4
  16.3 3.1 %nest_second.1 = (bf16[4,256,512]{2,1,0:T(8,128)(2,1)S(1)}, bf16[2,256,512]{2,1,0:T(8,128)(2,1)S(1)}, bf16[2,256,512]{2,1,0:T(8,128)(2,1)S(1)}, bf16[2,256,512]{...) custom-call(s32[1]{0:T(128)} %bitcast.y_ref, ...), custom_call_target="tpu_custom_call" | custom-call | flops 10485760 | bytes 10485760 | tf_op jit(solution)/shard_map/nest_second/pallas_call | solution.py:105
  19.4 2.0 %collective-permute-start.8 = (bf16[4,256,512]{2,1,0:T(8,128)(2,1)S(1)}, bf16[4,256,512]{2,1,0:T(8,128)(2,1)S(1)}, u32[]{:S(2)}, u32[]{:S(2)}) collective-permute-start(bf16[4,256,512]{2,1,0:T(8,128)(2,1)S(1)} %get-tuple-element.56.a_ref), channel_id=1, source_target_pairs={{0,2},{1,3},{2,0},{3,1},{4,6},{5,7},{6,4},{7,5},{8,10},{9,11},{10,... | collective-permute-start | bytes 3145736 | tf_op jit(solution)/shard_map/ppermute | solution.py:288
  21.4 4.5 %collective-permute-done.2.refs_1_.refs_3_ = bf16[2,256,512]{2,1,0:T(8,128)(2,1)S(1)} collective-permute-done((bf16[2,256,512]{2,1,0:T(8,128)(2,1)S(1)}, bf16[2,256,512]{2,1,0:T(8,128)(2,1)S(1)}, u32[]{:S(2)}, u32[]{:S(2)}) %collective-permute-start.2) | collective-permute-done | bytes 524320 | tf_op jit(solution)/shard_map/ppermute | solution.py:293
  25.9 12.4 %collective-permute-done.3.refs_2_.refs_4_ = bf16[2,256,512]{2,1,0:T(8,128)(2,1)S(1)} collective-permute-done((bf16[2,256,512]{2,1,0:T(8,128)(2,1)S(1)}, bf16[2,256,512]{2,1,0:T(8,128)(2,1)S(1)}, u32[]{:S(2)}, u32[]{:S(2)}) %collective-permute-start.3) | collective-permute-done | bytes 524320 | tf_op jit(solution)/shard_map/ppermute | solution.py:293
  38.3 1.2 partial_gram.2.refs_0_
  40.8 2.4 %collective-permute-start.6 = (bf16[2,256,512]{2,1,0:T(8,128)(2,1)S(1)}, bf16[2,256,512]{2,1,0:T(8,128)(2,1)S(1)}, u32[]{:S(2)}, u32[]{:S(2)}) collective-permute-start(bf16[2,256,512]{2,1,0:T(8,128)(2,1)S(1)} %get-tuple-element.63), channel_id=1, source_target_pairs={{0,128},{32,160},{64,192},{96,224},{128,0},{160,32},{192,64},{224,... | collective-permute-start | bytes 1572872 | tf_op jit(solution)/shard_map/ppermute | solution.py:293
  43.2 1.7 collective-permute-start.7
  44.9 5.4 %collective-permute-start.11 = (bf16[2,528,256]{2,1,0:T(8,128)(2,1)S(1)}, bf16[2,528,256]{2,1,0:T(8,128)(2,1)S(1)}, u32[]{:S(2)}, u32[]{:S(2)}) collective-permute-start(bf16[2,528,256]{2,1,0:T(8,128)(2,1)S(1)} %partial_gram.2.refs_0_), channel_id=1, source_target_pairs={{0,32},{32,0},{64,96},{96,64},{128,160},{160,128},{192,224},{224,1... | collective-permute-start | bytes 1622024 | tf_op jit(solution)/shard_map/ppermute | solution.py:288
  51.3 3.2 %collective-permute-done.5.refs_1_.refs_3_ = bf16[2,256,512]{2,1,0:T(8,128)(2,1)S(1)} collective-permute-done((bf16[2,256,512]{2,1,0:T(8,128)(2,1)S(1)}, bf16[2,256,512]{2,1,0:T(8,128)(2,1)S(1)}, u32[]{:S(2)}, u32[]{:S(2)}) %collective-permute-start.5) | collective-permute-done | bytes 524320 | tf_op jit(solution)/shard_map/ppermute | solution.py:293
  54.4 11.8 %collective-permute-done.6.refs_2_.refs_4_ = bf16[2,256,512]{2,1,0:T(8,128)(2,1)S(1)} collective-permute-done((bf16[2,256,512]{2,1,0:T(8,128)(2,1)S(1)}, bf16[2,256,512]{2,1,0:T(8,128)(2,1)S(1)}, u32[]{:S(2)}, u32[]{:S(2)}) %collective-permute-start.6) | collective-permute-done | bytes 524320 | tf_op jit(solution)/shard_map/ppermute | solution.py:293
  67.5 5.7 %collective-permute-start.9 = (bf16[2,528,256]{2,1,0:T(8,128)(2,1)S(1)}, bf16[2,528,256]{2,1,0:T(8,128)(2,1)S(1)}, u32[]{:S(2)}, u32[]{:S(2)}) collective-permute-start(bf16[2,528,256]{2,1,0:T(8,128)(2,1)S(1)} %partial_gram.3.refs_0_), channel_id=1, source_target_pairs={{0,32},{32,0},{64,96},{96,64},{128,160},{160,128},{192,224},{224,1... | collective-permute-start | bytes 1622024 | tf_op jit(solution)/shard_map/ppermute | solution.py:288
  73.7 8.2 %newton_schulz.2 = (bf16[2,256,512]{2,1,0:T(8,128)(2,1)S(1)}, bf16[2,256,512]{2,1,0:T(8,128)(2,1)S(1)}, bf16[2,256,512]{2,1,0:T(8,128)(2,1)S(1)}, bf16[2,256,512]{2,1,0:T(8,128)(2,1)S(1)}) custom-call(bf16[2,528,256]{2,1,0:T(8,128)(2,1)S(1)} %partial_gram.2.refs_0_, bf16[2,528,256]{2,1,0:T(8,128)(2,1)S(1)} %collective-permute-done.11.refs_1_, ...), custom_call_target="tpu_custom_call" | custom-call | flops 6979321856 | bytes 8388608 | tf_op jit(solution)/shard_map/newton_schulz/pallas_call | solution.py:226
  82.6 4.5 %collective-permute-done.10.b_ref = bf16[2,256,512]{2,1,0:T(8,128)(2,1)S(1)} collective-permute-done((bf16[2,256,512]{2,1,0:T(8,128)(2,1)S(1)}, bf16[2,256,512]{2,1,0:T(8,128)(2,1)S(1)}, u32[]{:S(2)}, u32[]{:S(2)}) %collective-permute-start.10) | collective-permute-done | bytes 524320 | tf_op jit(solution)/shard_map/ppermute | solution.py:288
  87.1 20.4 %collective-permute-done.9.refs_1_ = bf16[2,528,256]{2,1,0:T(8,128)(2,1)S(1)} collective-permute-done((bf16[2,528,256]{2,1,0:T(8,128)(2,1)S(1)}, bf16[2,528,256]{2,1,0:T(8,128)(2,1)S(1)}, u32[]{:S(2)}, u32[]{:S(2)}) %collective-permute-start.9) | collective-permute-done | bytes 540704 | tf_op jit(solution)/shard_map/ppermute | solution.py:288
  107.5 8.6 %newton_schulz.3 = (bf16[2,256,512]{2,1,0:T(8,128)(2,1)S(1)}, bf16[2,256,512]{2,1,0:T(8,128)(2,1)S(1)}, bf16[2,256,512]{2,1,0:T(8,128)(2,1)S(1)}, bf16[2,256,512]{2,1,0:T(8,128)(2,1)S(1)}) custom-call(bf16[2,528,256]{2,1,0:T(8,128)(2,1)S(1)} %partial_gram.3.refs_0_, bf16[2,528,256]{2,1,0:T(8,128)(2,1)S(1)} %collective-permute-done.9.refs_1_, ...), custom_call_target="tpu_custom_call" | custom-call | flops 6979321856 | bytes 8388608 | tf_op jit(solution)/shard_map/newton_schulz/pallas_call | solution.py:226
  116.5 1.7 collective-permute-start.17
  118.5 2.1 %collective-permute-start.19 = (bf16[2,256,512]{2,1,0:T(8,128)(2,1)S(1)}, bf16[2,256,512]{2,1,0:T(8,128)(2,1)S(1)}, u32[]{:S(2)}, u32[]{:S(2)}) collective-permute-start(bf16[2,256,512]{2,1,0:T(8,128)(2,1)S(1)} %local_params.4.a_ref), channel_id=1, source_target_pairs={{0,2},{1,3},{2,0},{3,1},{4,6},{5,7},{6,4},{7,5},{8,10},{9,11},{10,... | collective-permute-start | bytes 1572872 | tf_op jit(solution)/shard_map/ppermute | solution.py:288
  120.7 1.3 collective-permute-start.16
  121.9 9.2 %collective-permute-done.18.w_ref = bf16[2,256,512]{2,1,0:T(8,128)(2,1)S(1)} collective-permute-done((bf16[2,256,512]{2,1,0:T(8,128)(2,1)S(1)}, bf16[2,256,512]{2,1,0:T(8,128)(2,1)S(1)}, u32[]{:S(2)}, u32[]{:S(2)}) %collective-permute-start.18) | collective-permute-done | bytes 524320 | tf_op jit(solution)/shard_map/ppermute | solution.py:293
  131.4 10.4 %collective-permute-done.17.w_ref = bf16[2,256,512]{2,1,0:T(8,128)(2,1)S(1)} collective-permute-done((bf16[2,256,512]{2,1,0:T(8,128)(2,1)S(1)}, bf16[2,256,512]{2,1,0:T(8,128)(2,1)S(1)}, u32[]{:S(2)}, u32[]{:S(2)}) %collective-permute-start.17) | collective-permute-done | bytes 524320 | tf_op jit(solution)/shard_map/ppermute | solution.py:293
  142.6 1.9 %collective-permute-start.22 = (bf16[2,256,512]{2,1,0:T(8,128)(2,1)S(1)}, bf16[2,256,512]{2,1,0:T(8,128)(2,1)S(1)}, u32[]{:S(2)}, u32[]{:S(2)}) collective-permute-start(bf16[2,256,512]{2,1,0:T(8,128)(2,1)S(1)} %local_params.6.a_ref), channel_id=1, source_target_pairs={{0,2},{1,3},{2,0},{3,1},{4,6},{5,7},{6,4},{7,5},{8,10},{9,11},{10,... | collective-permute-start | bytes 1572872 | tf_op jit(solution)/shard_map/ppermute | solution.py:288
  144.7 1.7 replica_mean.7.refs_0_
  149.0 8.4 %collective-permute-done.21.b_ref = bf16[2,256,512]{2,1,0:T(8,128)(2,1)S(1)} collective-permute-done((bf16[2,256,512]{2,1,0:T(8,128)(2,1)S(1)}, bf16[2,256,512]{2,1,0:T(8,128)(2,1)S(1)}, u32[]{:S(2)}, u32[]{:S(2)}) %collective-permute-start.21) | collective-permute-done | bytes 524320 | tf_op jit(solution)/shard_map/ppermute | solution.py:288
  157.4 11.2 %collective-permute-done.22.b_ref = bf16[2,256,512]{2,1,0:T(8,128)(2,1)S(1)} collective-permute-done((bf16[2,256,512]{2,1,0:T(8,128)(2,1)S(1)}, bf16[2,256,512]{2,1,0:T(8,128)(2,1)S(1)}, u32[]{:S(2)}, u32[]{:S(2)}) %collective-permute-start.22) | collective-permute-done | bytes 524320 | tf_op jit(solution)/shard_map/ppermute | solution.py:288
  168.6 7.9 %collective-permute-done.23.b_ref = bf16[2,256,512]{2,1,0:T(8,128)(2,1)S(1)} collective-permute-done((bf16[2,256,512]{2,1,0:T(8,128)(2,1)S(1)}, bf16[2,256,512]{2,1,0:T(8,128)(2,1)S(1)}, u32[]{:S(2)}, u32[]{:S(2)}) %collective-permute-start.23) | collective-permute-done | bytes 524320 | tf_op jit(solution)/shard_map/ppermute | solution.py:288
  (41 shorter events, 12.2 us)
Async XLA Ops:
  0.6 2.2 %copy-start.1 = (bf16[2,1,8,256,512]{4,3,2,1,0:T(8,128)(2,1)S(1)}, bf16[2,1,8,256,512]{4,3,2,1,0:T(8,128)(2,1)}, u32[]{:S(2)}) copy-start(bf16[2,1,8,256,512]{4,3,2,1,0:T(8,128)(2,1)} %g_ref.3) | copy-start | bytes 12582916
  2.8 1.6 copy-start.3
  4.4 5.9 %copy-start = (bf16[1,8,256,512]{3,2,1,0:T(8,128)(2,1)S(1)}, bf16[1,8,256,512]{3,2,1,0:T(8,128)(2,1)}, u32[]{:S(2)}) copy-start(bf16[1,8,256,512]{3,2,1,0:T(8,128)(2,1)} %param.3) | copy-start | bytes 6291460
  4.4 11.8 %copy-start.2 = (bf16[2,1,8,256,512]{4,3,2,1,0:T(8,128)(2,1)S(1)}, bf16[2,1,8,256,512]{4,3,2,1,0:T(8,128)(2,1)}, u32[]{:S(2)}) copy-start(bf16[2,1,8,256,512]{4,3,2,1,0:T(8,128)(2,1)} %g_ref.3) | copy-start | bytes 12582916
  6.0 4.2 %collective-permute-start = (bf16[8,256,512]{2,1,0:T(8,128)(2,1)S(1)}, bf16[8,256,512]{2,1,0:T(8,128)(2,1)S(1)}, u32[]{:S(2)}, u32[]{:S(2)}) collective-permute-start(bf16[8,256,512]{2,1,0:T(8,128)(2,1)S(1)} %get-tuple-element.46.m_ref), channel_id=1, source_target_pairs={{0,1},{1,0},{2,3},{3,2},{4,5},{5,4},{6,7},{7,6},{8,9},{9,8},{10,11... | collective-permute-start | bytes 6291464 | tf_op jit(solution)/shard_map/ppermute | solution.py:288
  10.3 28.0 %collective-permute-start.1 = (bf16[8,256,512]{2,1,0:T(8,128)(2,1)S(1)}, bf16[8,256,512]{2,1,0:T(8,128)(2,1)S(1)}, u32[]{:S(2)}, u32[]{:S(2)}) collective-permute-start(bf16[8,256,512]{2,1,0:T(8,128)(2,1)S(1)} %bitcast.5), channel_id=1, source_target_pairs={{0,1},{1,0},{2,3},{3,2},{4,5},{5,4},{6,7},{7,6},{8,9},{9,8},{10,11... | collective-permute-start | bytes 6291464 | tf_op jit(solution)/shard_map/ppermute | solution.py:288
  10.4 15.5 %collective-permute-start.2 = (bf16[2,256,512]{2,1,0:T(8,128)(2,1)S(1)}, bf16[2,256,512]{2,1,0:T(8,128)(2,1)S(1)}, u32[]{:S(2)}, u32[]{:S(2)}) collective-permute-start(bf16[2,256,512]{2,1,0:T(8,128)(2,1)S(1)} %get-tuple-element.53), channel_id=1, source_target_pairs={{0,64},{32,96},{64,128},{96,160},{128,192},{160,224},{192,0},{224,... | collective-permute-start | bytes 1572872 | tf_op jit(solution)/shard_map/ppermute | solution.py:293
  12.0 26.3 %collective-permute-start.3 = (bf16[2,256,512]{2,1,0:T(8,128)(2,1)S(1)}, bf16[2,256,512]{2,1,0:T(8,128)(2,1)S(1)}, u32[]{:S(2)}, u32[]{:S(2)}) collective-permute-start(bf16[2,256,512]{2,1,0:T(8,128)(2,1)S(1)} %get-tuple-element.54), channel_id=1, source_target_pairs={{0,128},{32,160},{64,192},{96,224},{128,0},{160,32},{192,64},{224,... | collective-permute-start | bytes 1572872 | tf_op jit(solution)/shard_map/ppermute | solution.py:293
  14.9 23.4 %collective-permute-start.4 = (bf16[2,256,512]{2,1,0:T(8,128)(2,1)S(1)}, bf16[2,256,512]{2,1,0:T(8,128)(2,1)S(1)}, u32[]{:S(2)}, u32[]{:S(2)}) collective-permute-start(bf16[2,256,512]{2,1,0:T(8,128)(2,1)S(1)} %get-tuple-element.55), channel_id=1, source_target_pairs={{0,192},{32,224},{64,0},{96,32},{128,64},{160,96},{192,128},{224,1... | collective-permute-start | bytes 1572872 | tf_op jit(solution)/shard_map/ppermute | solution.py:293
  19.4 30.9 %collective-permute-start.8 = (bf16[4,256,512]{2,1,0:T(8,128)(2,1)S(1)}, bf16[4,256,512]{2,1,0:T(8,128)(2,1)S(1)}, u32[]{:S(2)}, u32[]{:S(2)}) collective-permute-start(bf16[4,256,512]{2,1,0:T(8,128)(2,1)S(1)} %get-tuple-element.56.a_ref), channel_id=1, source_target_pairs={{0,2},{1,3},{2,0},{3,1},{4,6},{5,7},{6,4},{7,5},{8,10},{9,11},{10,... | collective-permute-start | bytes 3145736 | tf_op jit(solution)/shard_map/ppermute | solution.py:288
  39.6 14.9 %collective-permute-start.5 = (bf16[2,256,512]{2,1,0:T(8,128)(2,1)S(1)}, bf16[2,256,512]{2,1,0:T(8,128)(2,1)S(1)}, u32[]{:S(2)}, u32[]{:S(2)}) collective-permute-start(bf16[2,256,512]{2,1,0:T(8,128)(2,1)S(1)} %get-tuple-element.62), channel_id=1, source_target_pairs={{0,64},{32,96},{64,128},{96,160},{128,192},{160,224},{192,0},{224,... | collective-permute-start | bytes 1572872 | tf_op jit(solution)/shard_map/ppermute | solution.py:293
  40.8 25.4 %collective-permute-start.6 = (bf16[2,256,512]{2,1,0:T(8,128)(2,1)S(1)}, bf16[2,256,512]{2,1,0:T(8,128)(2,1)S(1)}, u32[]{:S(2)}, u32[]{:S(2)}) collective-permute-start(bf16[2,256,512]{2,1,0:T(8,128)(2,1)S(1)} %get-tuple-element.63), channel_id=1, source_target_pairs={{0,128},{32,160},{64,192},{96,224},{128,0},{160,32},{192,64},{224,... | collective-permute-start | bytes 1572872 | tf_op jit(solution)/shard_map/ppermute | solution.py:293
  43.2 23.1 %collective-permute-start.7 = (bf16[2,256,512]{2,1,0:T(8,128)(2,1)S(1)}, bf16[2,256,512]{2,1,0:T(8,128)(2,1)S(1)}, u32[]{:S(2)}, u32[]{:S(2)}) collective-permute-start(bf16[2,256,512]{2,1,0:T(8,128)(2,1)S(1)} %get-tuple-element.64), channel_id=1, source_target_pairs={{0,192},{32,224},{64,0},{96,32},{128,64},{160,96},{192,128},{224,1... | collective-permute-start | bytes 1572872 | tf_op jit(solution)/shard_map/ppermute | solution.py:293
  44.9 28.9 %collective-permute-start.11 = (bf16[2,528,256]{2,1,0:T(8,128)(2,1)S(1)}, bf16[2,528,256]{2,1,0:T(8,128)(2,1)S(1)}, u32[]{:S(2)}, u32[]{:S(2)}) collective-permute-start(bf16[2,528,256]{2,1,0:T(8,128)(2,1)S(1)} %partial_gram.2.refs_0_), channel_id=1, source_target_pairs={{0,32},{32,0},{64,96},{96,64},{128,160},{160,128},{192,224},{224,1... | collective-permute-start | bytes 1622024 | tf_op jit(solution)/shard_map/ppermute | solution.py:288
  50.3 36.9 %collective-permute-start.10 = (bf16[2,256,512]{2,1,0:T(8,128)(2,1)S(1)}, bf16[2,256,512]{2,1,0:T(8,128)(2,1)S(1)}, u32[]{:S(2)}, u32[]{:S(2)}) collective-permute-start(bf16[2,256,512]{2,1,0:T(8,128)(2,1)S(1)} %get-tuple-element.70.a_ref), channel_id=1, source_target_pairs={{0,2},{1,3},{2,0},{3,1},{4,6},{5,7},{6,4},{7,5},{8,10},{9,11},{10,... | collective-permute-start | bytes 1572872 | tf_op jit(solution)/shard_map/ppermute | solution.py:288
  67.5 40.0 %collective-permute-start.9 = (bf16[2,528,256]{2,1,0:T(8,128)(2,1)S(1)}, bf16[2,528,256]{2,1,0:T(8,128)(2,1)S(1)}, u32[]{:S(2)}, u32[]{:S(2)}) collective-permute-start(bf16[2,528,256]{2,1,0:T(8,128)(2,1)S(1)} %partial_gram.3.refs_0_), channel_id=1, source_target_pairs={{0,32},{32,0},{64,96},{96,64},{128,160},{160,128},{192,224},{224,1... | collective-permute-start | bytes 1622024 | tf_op jit(solution)/shard_map/ppermute | solution.py:288
  81.9 25.5 %collective-permute-start.12 = (bf16[2,256,512]{2,1,0:T(8,128)(2,1)S(1)}, bf16[2,256,512]{2,1,0:T(8,128)(2,1)S(1)}, u32[]{:S(2)}, u32[]{:S(2)}) collective-permute-start(bf16[2,256,512]{2,1,0:T(8,128)(2,1)S(1)} %get-tuple-element.73.refs_6_), channel_id=1, source_target_pairs={{0,1},{1,0},{2,3},{3,2},{4,5},{5,4},{6,7},{7,6},{8,9},{9,8},{10,11... | collective-permute-start | bytes 1572872 | tf_op jit(solution)/shard_map/ppermute | solution.py:288
  82.0 25.5 %collective-permute-start.13 = (bf16[2,256,512]{2,1,0:T(8,128)(2,1)S(1)}, bf16[2,256,512]{2,1,0:T(8,128)(2,1)S(1)}, u32[]{:S(2)}, u32[]{:S(2)}) collective-permute-start(bf16[2,256,512]{2,1,0:T(8,128)(2,1)S(1)} %get-tuple-element.74.refs_7_), channel_id=1, source_target_pairs={{0,1},{1,0},{2,3},{3,2},{4,5},{5,4},{6,7},{7,6},{8,9},{9,8},{10,11... | collective-permute-start | bytes 1572872 | tf_op jit(solution)/shard_map/ppermute | solution.py:288
  82.5 25.0 %collective-permute-start.14 = (bf16[2,256,512]{2,1,0:T(8,128)(2,1)S(1)}, bf16[2,256,512]{2,1,0:T(8,128)(2,1)S(1)}, u32[]{:S(2)}, u32[]{:S(2)}) collective-permute-start(bf16[2,256,512]{2,1,0:T(8,128)(2,1)S(1)} %get-tuple-element.75.refs_8_), channel_id=1, source_target_pairs={{0,1},{1,0},{2,3},{3,2},{4,5},{5,4},{6,7},{7,6},{8,9},{9,8},{10,11... | collective-permute-start | bytes 1572872 | tf_op jit(solution)/shard_map/ppermute | solution.py:288
  87.1 20.4 %collective-permute-start.15 = (bf16[2,256,512]{2,1,0:T(8,128)(2,1)S(1)}, bf16[2,256,512]{2,1,0:T(8,128)(2,1)S(1)}, u32[]{:S(2)}, u32[]{:S(2)}) collective-permute-start(bf16[2,256,512]{2,1,0:T(8,128)(2,1)S(1)} %get-tuple-element.76.refs_9_), channel_id=1, source_target_pairs={{0,1},{1,0},{2,3},{3,2},{4,5},{5,4},{6,7},{7,6},{8,9},{9,8},{10,11... | collective-permute-start | bytes 1572872 | tf_op jit(solution)/shard_map/ppermute | solution.py:288
  116.1 14.9 %collective-permute-start.18 = (bf16[2,256,512]{2,1,0:T(8,128)(2,1)S(1)}, bf16[2,256,512]{2,1,0:T(8,128)(2,1)S(1)}, u32[]{:S(2)}, u32[]{:S(2)}) collective-permute-start(bf16[2,256,512]{2,1,0:T(8,128)(2,1)S(1)} %get-tuple-element.79), channel_id=1, source_target_pairs={{0,192},{32,224},{64,0},{96,32},{128,64},{160,96},{192,128},{224,1... | collective-permute-start | bytes 1572872 | tf_op jit(solution)/shard_map/ppermute | solution.py:293
  116.5 25.2 %collective-permute-start.17 = (bf16[2,256,512]{2,1,0:T(8,128)(2,1)S(1)}, bf16[2,256,512]{2,1,0:T(8,128)(2,1)S(1)}, u32[]{:S(2)}, u32[]{:S(2)}) collective-permute-start(bf16[2,256,512]{2,1,0:T(8,128)(2,1)S(1)} %get-tuple-element.78), channel_id=1, source_target_pairs={{0,64},{32,96},{64,128},{96,160},{128,192},{160,224},{192,0},{224,... | collective-permute-start | bytes 1572872 | tf_op jit(solution)/shard_map/ppermute | solution.py:293
  118.3 23.8 %collective-permute-start.20 = (bf16[2,256,512]{2,1,0:T(8,128)(2,1)S(1)}, bf16[2,256,512]{2,1,0:T(8,128)(2,1)S(1)}, u32[]{:S(2)}, u32[]{:S(2)}) collective-permute-start(bf16[2,256,512]{2,1,0:T(8,128)(2,1)S(1)} %get-tuple-element.84.a_ref), channel_id=1, source_target_pairs={{0,2},{1,3},{2,0},{3,1},{4,6},{5,7},{6,4},{7,5},{8,10},{9,11},{10,... | collective-permute-start | bytes 1572872 | tf_op jit(solution)/shard_map/ppermute | solution.py:288
  118.5 23.5 %collective-permute-start.19 = (bf16[2,256,512]{2,1,0:T(8,128)(2,1)S(1)}, bf16[2,256,512]{2,1,0:T(8,128)(2,1)S(1)}, u32[]{:S(2)}, u32[]{:S(2)}) collective-permute-start(bf16[2,256,512]{2,1,0:T(8,128)(2,1)S(1)} %local_params.4.a_ref), channel_id=1, source_target_pairs={{0,2},{1,3},{2,0},{3,1},{4,6},{5,7},{6,4},{7,5},{8,10},{9,11},{10,... | collective-permute-start | bytes 1572872 | tf_op jit(solution)/shard_map/ppermute | solution.py:288
  120.7 21.4 %collective-permute-start.16 = (bf16[2,256,512]{2,1,0:T(8,128)(2,1)S(1)}, bf16[2,256,512]{2,1,0:T(8,128)(2,1)S(1)}, u32[]{:S(2)}, u32[]{:S(2)}) collective-permute-start(bf16[2,256,512]{2,1,0:T(8,128)(2,1)S(1)} %get-tuple-element.77), channel_id=1, source_target_pairs={{0,128},{32,160},{64,192},{96,224},{128,0},{160,32},{192,64},{224,... | collective-permute-start | bytes 1572872 | tf_op jit(solution)/shard_map/ppermute | solution.py:293
  142.4 14.9 %collective-permute-start.21 = (bf16[2,256,512]{2,1,0:T(8,128)(2,1)S(1)}, bf16[2,256,512]{2,1,0:T(8,128)(2,1)S(1)}, u32[]{:S(2)}, u32[]{:S(2)}) collective-permute-start(bf16[2,256,512]{2,1,0:T(8,128)(2,1)S(1)} %local_params.7.a_ref), channel_id=1, source_target_pairs={{0,2},{1,3},{2,0},{3,1},{4,6},{5,7},{6,4},{7,5},{8,10},{9,11},{10,... | collective-permute-start | bytes 1572872 | tf_op jit(solution)/shard_map/ppermute | solution.py:288
  142.6 26.0 %collective-permute-start.22 = (bf16[2,256,512]{2,1,0:T(8,128)(2,1)S(1)}, bf16[2,256,512]{2,1,0:T(8,128)(2,1)S(1)}, u32[]{:S(2)}, u32[]{:S(2)}) collective-permute-start(bf16[2,256,512]{2,1,0:T(8,128)(2,1)S(1)} %local_params.6.a_ref), channel_id=1, source_target_pairs={{0,2},{1,3},{2,0},{3,1},{4,6},{5,7},{6,4},{7,5},{8,10},{9,11},{10,... | collective-permute-start | bytes 1572872 | tf_op jit(solution)/shard_map/ppermute | solution.py:288
  144.6 32.0 %collective-permute-start.23 = (bf16[2,256,512]{2,1,0:T(8,128)(2,1)S(1)}, bf16[2,256,512]{2,1,0:T(8,128)(2,1)S(1)}, u32[]{:S(2)}, u32[]{:S(2)}) collective-permute-start(bf16[2,256,512]{2,1,0:T(8,128)(2,1)S(1)} %local_params.5.a_ref), channel_id=1, source_target_pairs={{0,2},{1,3},{2,0},{3,1},{4,6},{5,7},{6,4},{7,5},{8,10},{9,11},{10,... | collective-permute-start | bytes 1572872 | tf_op jit(solution)/shard_map/ppermute | solution.py:288

commit v3 on v2

--- a/solution.py
+++ b/solution.py
@@ -27,7 +27,7 @@
 F32 = jnp.float32
 BF16 = jnp.bfloat16
 PAIR = jax.ShapeDtypeStruct((2, PART, COLS), BF16)
-FOUR = jax.ShapeDtypeStruct((4, PART, COLS), BF16)
+SIX = jax.ShapeDtypeStruct((6, PART, COLS), BF16)
 WHOLE = jax.ShapeDtypeStruct((MATS, PART, COLS), BF16)
 BLOCK = (1, PART, COLS)
 MIB = 1 << 20
@@ -97,8 +97,8 @@
     for d in range(4):
         @pl.when(t // 2 == d)
         def _():
-            out_refs[max(d - 1, 0)][0] = m_new
-            out_refs[3 + d][0] = nest
+            out_refs[d // 3][0] = m_new
+            out_refs[2 + d][0] = nest
 
 
 def second_step(y, m_new, m_peer, grads):
@@ -112,9 +112,9 @@
                 pl.BlockSpec(BLOCK, natural),
                 pl.BlockSpec((1, 1, 1, PART, COLS), lambda t, y_ref: (1, 0, mat_of(t, y_ref), 0, 0)),
             ],
-            out_specs=[run_of(0, 4)] + [group_spec(d) for d in (2, 3, 0, 1, 2, 3)],
-        ),
-        out_shape=[FOUR] + [PAIR] * 6,
+            out_specs=[run_of(0, 6), run_of(6, 2)] + [group_spec(d) for d in range(4)],
+        ),
+        out_shape=[SIX] + [PAIR] * 5,
         compiler_params=params_of(16),
         cost_estimate=cost(10 * MIB, 10 * MIB),
         name="nest_second",
@@ -309,23 +309,23 @@
     peer0 = flip(new0, "replica", 1)
     p_peer = flip(after(params, peer0), "replica", 1)
     rows0 = gather_rows(nest0)
-    ma, mb, mc, *nest1 = second_step(y, new0, peer0, grads)
+    ma, mb, *nest1 = second_step(y, new0, peer0, grads)
     ma_peer = flip(ma, "replica", 2)
 
     rows0 = after(rows0, ma, p_peer)
     gram0 = gram(rows0)
     other0 = flip(gram0, "fsdp", 1)
     rows1 = gather_rows(after(nest1, gram0))
-    gram1 = gram(after(rows1, ma_peer))
+    gram1 = gram(rows1)
     other1 = flip(gram1, "fsdp", 1)
     mb_peer = flip(after(mb, gram0), "replica", 2)
 
     u_own = update(gram0, after(other0, gram1), rows0)
     u_peer = [flip(u, "replica", 1) for u in u_own]
 
-    mc_peer = flip(after(mc, other1), "replica", 2)
-    w = update(gram1, after(other1, mb_peer), rows1, u_own, u_peer)
-    back = [w[0]] + [shift(w[d], -d) for d in (1, 2, 3)]
+    w = update(gram1, after(other1, mb_peer, ma_peer), rows1, u_own, u_peer)
+    back = [w[0], shift(w[1], -1), None, shift(w[3], -3)]
+    back[2] = shift(after(w[2], back[1]), -2)
     p_own = [None] * 4
     a_peer = [None] * 4
     p_own[0] = local(y, 0, params, p_peer, back[0])
@@ -334,12 +334,11 @@
     a_peer[1] = flip(p_own[1], "replica", 2)
     p_own[3] = local(y, 3, params, p_peer, after(back[3], p_own[1]))
     a_peer[3] = flip(p_own[3], "replica", 2)
-    p_own[2] = local(y, 2, params, p_peer, after(back[2], p_own[3], a_peer[0], mc_peer))
+    p_own[2] = local(y, 2, params, p_peer, after(back[2], p_own[3], a_peer[0], a_peer[1]))
     a_peer[2] = flip(p_own[2], "replica", 2)
 
     m_out = mean_into(y, 0, ma, ma_peer, None)
-    m_out = mean_into(y, 2, mb, mb_peer, m_out)
-    m_out = mean_into(y, 3, mc, mc_peer, m_out)
+    m_out = mean_into(y, 3, mb, mb_peer, m_out)
     p_out = None
     for d in (0, 1, 3, 2):
         p_out = mean_into(y, d, p_own[d], after(a_peer[d], m_out), p_out)

time: 179 us -> 174 us (0.972)
  waiting for transfers between devices: 109 us -> 103 us
    ppermute x9, waiting for transfers between devices: 51.4 us -> 40.8 us  [shift(): lax.ppermute(value, 'fsdp', [(s, (s + 2 * d) % count) for s in range(coun...]
    ppermute x15 -> x14, waiting for transfers between devices: 57.1 us -> 62.3 us  [flip(): lax.ppermute(value, axis, [(s, s ^ mask) for s in range(lax.axis_size(axi...]
    ppermute x15 -> x14, starting transfers between devices: 19.3 us -> 20.3 us  [flip(): lax.ppermute(value, axis, [(s, s ^ mask) for s in range(lax.axis_size(axi...]
    pallas_call x7 -> x6, Pallas kernels: 7.04 us -> 6.91 us  [mean_into(): pl.pallas_call(mean_kernel, grid_spec=pltpu.PrefetchScalarGridSpec(num_sc...]
  transfers between devices with their start and end apart: 24 -> 23, of which waited for: 13 -> 13; matrix products, arithmetic and copies ran while one was open for 0% -> 0% of each run, Pallas kernels for 11% -> 12%
where the time goes in v3:
time: 174 us
  waiting for transfers between devices  103 us (59%)
  starting transfers between devices  34 us (20%)
  Pallas kernels  32.1 us (18%)
  local copies, waits for them, and re-layouts  3.78 us (2%)
    ppermute x14, waiting for transfers between devices, flip(): lax.ppermute(value, axis, [(s, s ^ mask) for s in range(lax.axis_size(axi...  62.3 us
    ppermute x9, waiting for transfers between devices, shift(): lax.ppermute(value, 'fsdp', [(s, (s + 2 * d) % count) for s in range(coun...  40.8 us
    ppermute x14, starting transfers between devices, flip(): lax.ppermute(value, axis, [(s, s ^ mask) for s in range(lax.axis_size(axi...  20.3 us
    pallas_call x2, Pallas kernels, update(): pl.pallas_call(functools.partial(update_kernel, last), in_specs=[pl.Block...  16.8 us
    ppermute x9, starting transfers between devices, shift(): lax.ppermute(value, 'fsdp', [(s, (s + 2 * d) % count) for s in range(coun...  13.7 us
    pallas_call x6, Pallas kernels, mean_into(): pl.pallas_call(mean_kernel, grid_spec=pltpu.PrefetchScalarGridSpec(num_sc...  6.91 us
    unnamed x8, local copies, waits for them, and re-layouts  3.78 us
  transfers between devices with their start and end apart: 23, of which 13 were waited for; matrix products, arithmetic and copies ran while one was open for 0% of the time, Pallas kernels for 12%

profile of v3, /device:TPU:66, one launch (start us, length us, event | category | flops | bytes accessed | tf_op | source)
XLA Modules:
  0.0 173.7 jit_solution(6559962715171831684)
XLA Ops:
  0.7 2.2 %copy-done.1 = bf16[2,1,8,256,512]{4,3,2,1,0:T(8,128)(2,1)S(1)} copy-done((bf16[2,1,8,256,512]{4,3,2,1,0:T(8,128)(2,1)S(1)}, bf16[2,1,8,256,512]{4,3,2,1,0:T(8,128)(2,1)}, u32[]{:S(2)}) %copy-start.1) | copy-done | bytes 4194328
  2.8 1.6 copy-done.3
  4.4 1.6 nest_first.1
  6.1 4.1 %collective-permute-done.peer_ref = bf16[8,256,512]{2,1,0:T(8,128)(2,1)S(1)} collective-permute-done((bf16[8,256,512]{2,1,0:T(8,128)(2,1)S(1)}, bf16[8,256,512]{2,1,0:T(8,128)(2,1)S(1)}, u32[]{:S(2)}, u32[]{:S(2)}) %collective-permute-start) | collective-permute-done | bytes 2097184 | tf_op jit(solution)/shard_map/ppermute | solution.py:288
  10.4 1.6 collective-permute-start.2
  12.0 2.9 %collective-permute-start.3 = (bf16[2,256,512]{2,1,0:T(8,128)(2,1)S(1)}, bf16[2,256,512]{2,1,0:T(8,128)(2,1)S(1)}, u32[]{:S(2)}, u32[]{:S(2)}) collective-permute-start(bf16[2,256,512]{2,1,0:T(8,128)(2,1)S(1)} %get-tuple-element.49), channel_id=1, source_target_pairs={{0,128},{32,160},{64,192},{96,224},{128,0},{160,32},{192,64},{224,... | collective-permute-start | bytes 1572872 | tf_op jit(solution)/shard_map/ppermute | solution.py:293
  14.9 1.3 collective-permute-start.4
  16.3 3.1 %nest_second.1 = (bf16[6,256,512]{2,1,0:T(8,128)(2,1)S(1)}, bf16[2,256,512]{2,1,0:T(8,128)(2,1)S(1)}, bf16[2,256,512]{2,1,0:T(8,128)(2,1)S(1)}, bf16[2,256,512]{...) custom-call(s32[1]{0:T(128)} %bitcast.y_ref, ...), custom_call_target="tpu_custom_call" | custom-call | flops 10485760 | bytes 10485760 | tf_op jit(solution)/shard_map/nest_second/pallas_call | solution.py:105
  19.4 2.0 %collective-permute-start.10 = (bf16[6,256,512]{2,1,0:T(8,128)(2,1)S(1)}, bf16[6,256,512]{2,1,0:T(8,128)(2,1)S(1)}, u32[]{:S(2)}, u32[]{:S(2)}) collective-permute-start(bf16[6,256,512]{2,1,0:T(8,128)(2,1)S(1)} %get-tuple-element.51.a_ref), channel_id=1, source_target_pairs={{0,2},{1,3},{2,0},{3,1},{4,6},{5,7},{6,4},{7,5},{8,10},{9,11},{10,... | collective-permute-start | bytes 4718600 | tf_op jit(solution)/shard_map/ppermute | solution.py:288
  21.4 4.5 %collective-permute-done.2.refs_1_.refs_3_ = bf16[2,256,512]{2,1,0:T(8,128)(2,1)S(1)} collective-permute-done((bf16[2,256,512]{2,1,0:T(8,128)(2,1)S(1)}, bf16[2,256,512]{2,1,0:T(8,128)(2,1)S(1)}, u32[]{:S(2)}, u32[]{:S(2)}) %collective-permute-start.2) | collective-permute-done | bytes 524320 | tf_op jit(solution)/shard_map/ppermute | solution.py:293
  25.9 12.4 %collective-permute-done.3.refs_2_.refs_4_ = bf16[2,256,512]{2,1,0:T(8,128)(2,1)S(1)} collective-permute-done((bf16[2,256,512]{2,1,0:T(8,128)(2,1)S(1)}, bf16[2,256,512]{2,1,0:T(8,128)(2,1)S(1)}, u32[]{:S(2)}, u32[]{:S(2)}) %collective-permute-start.3) | collective-permute-done | bytes 524320 | tf_op jit(solution)/shard_map/ppermute | solution.py:293
  38.3 1.2 partial_gram.2.refs_0_
  39.6 1.2 collective-permute-start.5
  40.8 2.4 %collective-permute-start.6 = (bf16[2,256,512]{2,1,0:T(8,128)(2,1)S(1)}, bf16[2,256,512]{2,1,0:T(8,128)(2,1)S(1)}, u32[]{:S(2)}, u32[]{:S(2)}) collective-permute-start(bf16[2,256,512]{2,1,0:T(8,128)(2,1)S(1)} %get-tuple-element.58), channel_id=1, source_target_pairs={{0,128},{32,160},{64,192},{96,224},{128,0},{160,32},{192,64},{224,... | collective-permute-start | bytes 1572872 | tf_op jit(solution)/shard_map/ppermute | solution.py:293
  43.2 1.7 collective-permute-start.7
  44.9 5.4 %collective-permute-start.11 = (bf16[2,528,256]{2,1,0:T(8,128)(2,1)S(1)}, bf16[2,528,256]{2,1,0:T(8,128)(2,1)S(1)}, u32[]{:S(2)}, u32[]{:S(2)}) collective-permute-start(bf16[2,528,256]{2,1,0:T(8,128)(2,1)S(1)} %partial_gram.2.refs_0_), channel_id=1, source_target_pairs={{0,32},{32,0},{64,96},{96,64},{128,160},{160,128},{192,224},{224,1... | collective-permute-start | bytes 1622024 | tf_op jit(solution)/shard_map/ppermute | solution.py:288
  50.3 4.2 %collective-permute-done.5.refs_1_.refs_3_ = bf16[2,256,512]{2,1,0:T(8,128)(2,1)S(1)} collective-permute-done((bf16[2,256,512]{2,1,0:T(8,128)(2,1)S(1)}, bf16[2,256,512]{2,1,0:T(8,128)(2,1)S(1)}, u32[]{:S(2)}, u32[]{:S(2)}) %collective-permute-start.5) | collective-permute-done | bytes 524320 | tf_op jit(solution)/shard_map/ppermute | solution.py:293
  54.4 1.9 %collective-permute-start.9 = (bf16[2,256,512]{2,1,0:T(8,128)(2,1)S(1)}, bf16[2,256,512]{2,1,0:T(8,128)(2,1)S(1)}, u32[]{:S(2)}, u32[]{:S(2)}) collective-permute-start(bf16[2,256,512]{2,1,0:T(8,128)(2,1)S(1)} %get-tuple-element.61.a_ref), channel_id=1, source_target_pairs={{0,2},{1,3},{2,0},{3,1},{4,6},{5,7},{6,4},{7,5},{8,10},{9,11},{10,... | collective-permute-start | bytes 1572872 | tf_op jit(solution)/shard_map/ppermute | solution.py:288
  56.4 9.9 %collective-permute-done.6.refs_2_.refs_4_ = bf16[2,256,512]{2,1,0:T(8,128)(2,1)S(1)} collective-permute-done((bf16[2,256,512]{2,1,0:T(8,128)(2,1)S(1)}, bf16[2,256,512]{2,1,0:T(8,128)(2,1)S(1)}, u32[]{:S(2)}, u32[]{:S(2)}) %collective-permute-start.6) | collective-permute-done | bytes 524320 | tf_op jit(solution)/shard_map/ppermute | solution.py:293
  66.2 1.2 partial_gram.3.refs_0_
  67.5 5.7 %collective-permute-start.8 = (bf16[2,528,256]{2,1,0:T(8,128)(2,1)S(1)}, bf16[2,528,256]{2,1,0:T(8,128)(2,1)S(1)}, u32[]{:S(2)}, u32[]{:S(2)}) collective-permute-start(bf16[2,528,256]{2,1,0:T(8,128)(2,1)S(1)} %partial_gram.3.refs_0_), channel_id=1, source_target_pairs={{0,32},{32,0},{64,96},{96,64},{128,160},{160,128},{192,224},{224,1... | collective-permute-start | bytes 1622024 | tf_op jit(solution)/shard_map/ppermute | solution.py:288
  73.2 10.9 %collective-permute-done.11.refs_1_ = bf16[2,528,256]{2,1,0:T(8,128)(2,1)S(1)} collective-permute-done((bf16[2,528,256]{2,1,0:T(8,128)(2,1)S(1)}, bf16[2,528,256]{2,1,0:T(8,128)(2,1)S(1)}, u32[]{:S(2)}, u32[]{:S(2)}) %collective-permute-start.11) | collective-permute-done | bytes 540704 | tf_op jit(solution)/shard_map/ppermute | solution.py:288
  84.1 8.2 %newton_schulz.2 = (bf16[2,256,512]{2,1,0:T(8,128)(2,1)S(1)}, bf16[2,256,512]{2,1,0:T(8,128)(2,1)S(1)}, bf16[2,256,512]{2,1,0:T(8,128)(2,1)S(1)}, bf16[2,256,512]{2,1,0:T(8,128)(2,1)S(1)}) custom-call(bf16[2,528,256]{2,1,0:T(8,128)(2,1)S(1)} %partial_gram.2.refs_0_, bf16[2,528,256]{2,1,0:T(8,128)(2,1)S(1)} %collective-permute-done.11.refs_1_, ...), custom_call_target="tpu_custom_call" | custom-call | flops 6979321856 | bytes 8388608 | tf_op jit(solution)/shard_map/newton_schulz/pallas_call | solution.py:226
  93.0 9.1 %collective-permute-done.9.b_ref = bf16[2,256,512]{2,1,0:T(8,128)(2,1)S(1)} collective-permute-done((bf16[2,256,512]{2,1,0:T(8,128)(2,1)S(1)}, bf16[2,256,512]{2,1,0:T(8,128)(2,1)S(1)}, u32[]{:S(2)}, u32[]{:S(2)}) %collective-permute-start.9) | collective-permute-done | bytes 524320 | tf_op jit(solution)/shard_map/ppermute | solution.py:288
  102.1 15.2 %collective-permute-done.8.refs_1_ = bf16[2,528,256]{2,1,0:T(8,128)(2,1)S(1)} collective-permute-done((bf16[2,528,256]{2,1,0:T(8,128)(2,1)S(1)}, bf16[2,528,256]{2,1,0:T(8,128)(2,1)S(1)}, u32[]{:S(2)}, u32[]{:S(2)}) %collective-permute-start.8) | collective-permute-done | bytes 540704 | tf_op jit(solution)/shard_map/ppermute | solution.py:288
  117.3 8.6 %newton_schulz.3 = (bf16[2,256,512]{2,1,0:T(8,128)(2,1)S(1)}, bf16[2,256,512]{2,1,0:T(8,128)(2,1)S(1)}, bf16[2,256,512]{2,1,0:T(8,128)(2,1)S(1)}, bf16[2,256,512]{2,1,0:T(8,128)(2,1)S(1)}) custom-call(bf16[2,528,256]{2,1,0:T(8,128)(2,1)S(1)} %partial_gram.3.refs_0_, bf16[2,528,256]{2,1,0:T(8,128)(2,1)S(1)} %collective-permute-done.8.refs_1_, ...), custom_call_target="tpu_custom_call" | custom-call | flops 6979321856 | bytes 8388608 | tf_op jit(solution)/shard_map/newton_schulz/pallas_call | solution.py:226
  127.7 1.7 %collective-permute-start.18 = (bf16[2,256,512]{2,1,0:T(8,128)(2,1)S(1)}, bf16[2,256,512]{2,1,0:T(8,128)(2,1)S(1)}, u32[]{:S(2)}, u32[]{:S(2)}) collective-permute-start(bf16[2,256,512]{2,1,0:T(8,128)(2,1)S(1)} %get-tuple-element.71), channel_id=1, source_target_pairs={{0,64},{32,96},{64,128},{96,160},{128,192},{160,224},{192,0},{224,... | collective-permute-start | bytes 1572872 | tf_op jit(solution)/shard_map/ppermute | solution.py:293
  129.4 9.0 %collective-permute-done.16.w_ref = bf16[2,256,512]{2,1,0:T(8,128)(2,1)S(1)} collective-permute-done((bf16[2,256,512]{2,1,0:T(8,128)(2,1)S(1)}, bf16[2,256,512]{2,1,0:T(8,128)(2,1)S(1)}, u32[]{:S(2)}, u32[]{:S(2)}) %collective-permute-start.16) | collective-permute-done | bytes 524320 | tf_op jit(solution)/shard_map/ppermute | solution.py:293
  142.5 11.2 %collective-permute-done.20.b_ref = bf16[2,256,512]{2,1,0:T(8,128)(2,1)S(1)} collective-permute-done((bf16[2,256,512]{2,1,0:T(8,128)(2,1)S(1)}, bf16[2,256,512]{2,1,0:T(8,128)(2,1)S(1)}, u32[]{:S(2)}, u32[]{:S(2)}) %collective-permute-start.20) | collective-permute-done | bytes 524320 | tf_op jit(solution)/shard_map/ppermute | solution.py:288
  155.1 2.5 %replica_mean.6.refs_0_ = bf16[8,256,512]{2,1,0:T(8,128)(2,1)} custom-call(s32[1]{0:T(128)} %bitcast.y_ref, bf16[6,256,512]{2,1,0:T(8,128)(2,1)S(1)} %get-tuple-element.51.a_ref, bf16[6,256,512]{2,1,0:T(8,128)(2,1)S(1)} %collective-permute-done.10.b_ref), custom_call_target="tpu_custom_call" | custom-call | flops 1048576 | bytes 2097152 | tf_op jit(solution)/shard_map/replica_mean/pallas_call | solution.py:271
  159.3 5.6 %collective-permute-done.22.b_ref = bf16[2,256,512]{2,1,0:T(8,128)(2,1)S(1)} collective-permute-done((bf16[2,256,512]{2,1,0:T(8,128)(2,1)S(1)}, bf16[2,256,512]{2,1,0:T(8,128)(2,1)S(1)}, u32[]{:S(2)}, u32[]{:S(2)}) %collective-permute-start.22) | collective-permute-done | bytes 524320 | tf_op jit(solution)/shard_map/ppermute | solution.py:288
  166.7 6.1 %collective-permute-done.21.b_ref = bf16[2,256,512]{2,1,0:T(8,128)(2,1)S(1)} collective-permute-done((bf16[2,256,512]{2,1,0:T(8,128)(2,1)S(1)}, bf16[2,256,512]{2,1,0:T(8,128)(2,1)S(1)}, u32[]{:S(2)}, u32[]{:S(2)}) %collective-permute-start.21) | collective-permute-done | bytes 524320 | tf_op jit(solution)/shard_map/ppermute | solution.py:288
  (38 shorter events, 12.6 us)
Async XLA Ops:
  0.6 2.2 %copy-start.1 = (bf16[2,1,8,256,512]{4,3,2,1,0:T(8,128)(2,1)S(1)}, bf16[2,1,8,256,512]{4,3,2,1,0:T(8,128)(2,1)}, u32[]{:S(2)}) copy-start(bf16[2,1,8,256,512]{4,3,2,1,0:T(8,128)(2,1)} %g_ref.3) | copy-start | bytes 12582916
  2.8 1.6 copy-start.3
  4.4 5.9 %copy-start = (bf16[1,8,256,512]{3,2,1,0:T(8,128)(2,1)S(1)}, bf16[1,8,256,512]{3,2,1,0:T(8,128)(2,1)}, u32[]{:S(2)}) copy-start(bf16[1,8,256,512]{3,2,1,0:T(8,128)(2,1)} %param.3) | copy-start | bytes 6291460
  4.4 11.8 %copy-start.2 = (bf16[2,1,8,256,512]{4,3,2,1,0:T(8,128)(2,1)S(1)}, bf16[2,1,8,256,512]{4,3,2,1,0:T(8,128)(2,1)}, u32[]{:S(2)}) copy-start(bf16[2,1,8,256,512]{4,3,2,1,0:T(8,128)(2,1)} %g_ref.3) | copy-start | bytes 12582916
  6.0 4.2 %collective-permute-start = (bf16[8,256,512]{2,1,0:T(8,128)(2,1)S(1)}, bf16[8,256,512]{2,1,0:T(8,128)(2,1)S(1)}, u32[]{:S(2)}, u32[]{:S(2)}) collective-permute-start(bf16[8,256,512]{2,1,0:T(8,128)(2,1)S(1)} %get-tuple-element.41.m_ref), channel_id=1, source_target_pairs={{0,1},{1,0},{2,3},{3,2},{4,5},{5,4},{6,7},{7,6},{8,9},{9,8},{10,11... | collective-permute-start | bytes 6291464 | tf_op jit(solution)/shard_map/ppermute | solution.py:288
  10.3 28.0 %collective-permute-start.1 = (bf16[8,256,512]{2,1,0:T(8,128)(2,1)S(1)}, bf16[8,256,512]{2,1,0:T(8,128)(2,1)S(1)}, u32[]{:S(2)}, u32[]{:S(2)}) collective-permute-start(bf16[8,256,512]{2,1,0:T(8,128)(2,1)S(1)} %bitcast.5), channel_id=1, source_target_pairs={{0,1},{1,0},{2,3},{3,2},{4,5},{5,4},{6,7},{7,6},{8,9},{9,8},{10,11... | collective-permute-start | bytes 6291464 | tf_op jit(solution)/shard_map/ppermute | solution.py:288
  10.4 15.5 %collective-permute-start.2 = (bf16[2,256,512]{2,1,0:T(8,128)(2,1)S(1)}, bf16[2,256,512]{2,1,0:T(8,128)(2,1)S(1)}, u32[]{:S(2)}, u32[]{:S(2)}) collective-permute-start(bf16[2,256,512]{2,1,0:T(8,128)(2,1)S(1)} %get-tuple-element.48), channel_id=1, source_target_pairs={{0,64},{32,96},{64,128},{96,160},{128,192},{160,224},{192,0},{224,... | collective-permute-start | bytes 1572872 | tf_op jit(solution)/shard_map/ppermute | solution.py:293
  12.0 26.3 %collective-permute-start.3 = (bf16[2,256,512]{2,1,0:T(8,128)(2,1)S(1)}, bf16[2,256,512]{2,1,0:T(8,128)(2,1)S(1)}, u32[]{:S(2)}, u32[]{:S(2)}) collective-permute-start(bf16[2,256,512]{2,1,0:T(8,128)(2,1)S(1)} %get-tuple-element.49), channel_id=1, source_target_pairs={{0,128},{32,160},{64,192},{96,224},{128,0},{160,32},{192,64},{224,... | collective-permute-start | bytes 1572872 | tf_op jit(solution)/shard_map/ppermute | solution.py:293
  14.9 23.4 %collective-permute-start.4 = (bf16[2,256,512]{2,1,0:T(8,128)(2,1)S(1)}, bf16[2,256,512]{2,1,0:T(8,128)(2,1)S(1)}, u32[]{:S(2)}, u32[]{:S(2)}) collective-permute-start(bf16[2,256,512]{2,1,0:T(8,128)(2,1)S(1)} %get-tuple-element.50), channel_id=1, source_target_pairs={{0,192},{32,224},{64,0},{96,32},{128,64},{160,96},{192,128},{224,1... | collective-permute-start | bytes 1572872 | tf_op jit(solution)/shard_map/ppermute | solution.py:293
  19.4 73.5 %collective-permute-start.10 = (bf16[6,256,512]{2,1,0:T(8,128)(2,1)S(1)}, bf16[6,256,512]{2,1,0:T(8,128)(2,1)S(1)}, u32[]{:S(2)}, u32[]{:S(2)}) collective-permute-start(bf16[6,256,512]{2,1,0:T(8,128)(2,1)S(1)} %get-tuple-element.51.a_ref), channel_id=1, source_target_pairs={{0,2},{1,3},{2,0},{3,1},{4,6},{5,7},{6,4},{7,5},{8,10},{9,11},{10,... | collective-permute-start | bytes 4718600 | tf_op jit(solution)/shard_map/ppermute | solution.py:288
  39.6 14.9 %collective-permute-start.5 = (bf16[2,256,512]{2,1,0:T(8,128)(2,1)S(1)}, bf16[2,256,512]{2,1,0:T(8,128)(2,1)S(1)}, u32[]{:S(2)}, u32[]{:S(2)}) collective-permute-start(bf16[2,256,512]{2,1,0:T(8,128)(2,1)S(1)} %get-tuple-element.57), channel_id=1, source_target_pairs={{0,64},{32,96},{64,128},{96,160},{128,192},{160,224},{192,0},{224,... | collective-permute-start | bytes 1572872 | tf_op jit(solution)/shard_map/ppermute | solution.py:293
  40.8 25.4 %collective-permute-start.6 = (bf16[2,256,512]{2,1,0:T(8,128)(2,1)S(1)}, bf16[2,256,512]{2,1,0:T(8,128)(2,1)S(1)}, u32[]{:S(2)}, u32[]{:S(2)}) collective-permute-start(bf16[2,256,512]{2,1,0:T(8,128)(2,1)S(1)} %get-tuple-element.58), channel_id=1, source_target_pairs={{0,128},{32,160},{64,192},{96,224},{128,0},{160,32},{192,64},{224,... | collective-permute-start | bytes 1572872 | tf_op jit(solution)/shard_map/ppermute | solution.py:293
  43.2 23.1 %collective-permute-start.7 = (bf16[2,256,512]{2,1,0:T(8,128)(2,1)S(1)}, bf16[2,256,512]{2,1,0:T(8,128)(2,1)S(1)}, u32[]{:S(2)}, u32[]{:S(2)}) collective-permute-start(bf16[2,256,512]{2,1,0:T(8,128)(2,1)S(1)} %get-tuple-element.59), channel_id=1, source_target_pairs={{0,192},{32,224},{64,0},{96,32},{128,64},{160,96},{192,128},{224,1... | collective-permute-start | bytes 1572872 | tf_op jit(solution)/shard_map/ppermute | solution.py:293
  44.9 39.2 %collective-permute-start.11 = (bf16[2,528,256]{2,1,0:T(8,128)(2,1)S(1)}, bf16[2,528,256]{2,1,0:T(8,128)(2,1)S(1)}, u32[]{:S(2)}, u32[]{:S(2)}) collective-permute-start(bf16[2,528,256]{2,1,0:T(8,128)(2,1)S(1)} %partial_gram.2.refs_0_), channel_id=1, source_target_pairs={{0,32},{32,0},{64,96},{96,64},{128,160},{160,128},{192,224},{224,1... | collective-permute-start | bytes 1622024 | tf_op jit(solution)/shard_map/ppermute | solution.py:288
  54.4 47.7 %collective-permute-start.9 = (bf16[2,256,512]{2,1,0:T(8,128)(2,1)S(1)}, bf16[2,256,512]{2,1,0:T(8,128)(2,1)S(1)}, u32[]{:S(2)}, u32[]{:S(2)}) collective-permute-start(bf16[2,256,512]{2,1,0:T(8,128)(2,1)S(1)} %get-tuple-element.61.a_ref), channel_id=1, source_target_pairs={{0,2},{1,3},{2,0},{3,1},{4,6},{5,7},{6,4},{7,5},{8,10},{9,11},{10,... | collective-permute-start | bytes 1572872 | tf_op jit(solution)/shard_map/ppermute | solution.py:288
  67.5 49.8 %collective-permute-start.8 = (bf16[2,528,256]{2,1,0:T(8,128)(2,1)S(1)}, bf16[2,528,256]{2,1,0:T(8,128)(2,1)S(1)}, u32[]{:S(2)}, u32[]{:S(2)}) collective-permute-start(bf16[2,528,256]{2,1,0:T(8,128)(2,1)S(1)} %partial_gram.3.refs_0_), channel_id=1, source_target_pairs={{0,32},{32,0},{64,96},{96,64},{128,160},{160,128},{192,224},{224,1... | collective-permute-start | bytes 1622024 | tf_op jit(solution)/shard_map/ppermute | solution.py:288
  92.3 25.0 %collective-permute-start.12 = (bf16[2,256,512]{2,1,0:T(8,128)(2,1)S(1)}, bf16[2,256,512]{2,1,0:T(8,128)(2,1)S(1)}, u32[]{:S(2)}, u32[]{:S(2)}) collective-permute-start(bf16[2,256,512]{2,1,0:T(8,128)(2,1)S(1)} %get-tuple-element.64.refs_6_), channel_id=1, source_target_pairs={{0,1},{1,0},{2,3},{3,2},{4,5},{5,4},{6,7},{7,6},{8,9},{9,8},{10,11... | collective-permute-start | bytes 1572872 | tf_op jit(solution)/shard_map/ppermute | solution.py:288
  92.4 24.9 %collective-permute-start.13 = (bf16[2,256,512]{2,1,0:T(8,128)(2,1)S(1)}, bf16[2,256,512]{2,1,0:T(8,128)(2,1)S(1)}, u32[]{:S(2)}, u32[]{:S(2)}) collective-permute-start(bf16[2,256,512]{2,1,0:T(8,128)(2,1)S(1)} %get-tuple-element.65.refs_7_), channel_id=1, source_target_pairs={{0,1},{1,0},{2,3},{3,2},{4,5},{5,4},{6,7},{7,6},{8,9},{9,8},{10,11... | collective-permute-start | bytes 1572872 | tf_op jit(solution)/shard_map/ppermute | solution.py:288
  92.9 24.4 %collective-permute-start.14 = (bf16[2,256,512]{2,1,0:T(8,128)(2,1)S(1)}, bf16[2,256,512]{2,1,0:T(8,128)(2,1)S(1)}, u32[]{:S(2)}, u32[]{:S(2)}) collective-permute-start(bf16[2,256,512]{2,1,0:T(8,128)(2,1)S(1)} %get-tuple-element.66.refs_8_), channel_id=1, source_target_pairs={{0,1},{1,0},{2,3},{3,2},{4,5},{5,4},{6,7},{7,6},{8,9},{9,8},{10,11... | collective-permute-start | bytes 1572872 | tf_op jit(solution)/shard_map/ppermute | solution.py:288
  102.1 15.2 %collective-permute-start.15 = (bf16[2,256,512]{2,1,0:T(8,128)(2,1)S(1)}, bf16[2,256,512]{2,1,0:T(8,128)(2,1)S(1)}, u32[]{:S(2)}, u32[]{:S(2)}) collective-permute-start(bf16[2,256,512]{2,1,0:T(8,128)(2,1)S(1)} %get-tuple-element.67.refs_9_), channel_id=1, source_target_pairs={{0,1},{1,0},{2,3},{3,2},{4,5},{5,4},{6,7},{7,6},{8,9},{9,8},{10,11... | collective-permute-start | bytes 1572872 | tf_op jit(solution)/shard_map/ppermute | solution.py:288
  125.9 12.5 %collective-permute-start.16 = (bf16[2,256,512]{2,1,0:T(8,128)(2,1)S(1)}, bf16[2,256,512]{2,1,0:T(8,128)(2,1)S(1)}, u32[]{:S(2)}, u32[]{:S(2)}) collective-permute-start(bf16[2,256,512]{2,1,0:T(8,128)(2,1)S(1)} %get-tuple-element.69), channel_id=1, source_target_pairs={{0,192},{32,224},{64,0},{96,32},{128,64},{160,96},{192,128},{224,1... | collective-permute-start | bytes 1572872 | tf_op jit(solution)/shard_map/ppermute | solution.py:293
  126.6 15.9 %collective-permute-start.19 = (bf16[2,256,512]{2,1,0:T(8,128)(2,1)S(1)}, bf16[2,256,512]{2,1,0:T(8,128)(2,1)S(1)}, u32[]{:S(2)}, u32[]{:S(2)}) collective-permute-start(bf16[2,256,512]{2,1,0:T(8,128)(2,1)S(1)} %local_params.4.a_ref), channel_id=1, source_target_pairs={{0,2},{1,3},{2,0},{3,1},{4,6},{5,7},{6,4},{7,5},{8,10},{9,11},{10,... | collective-permute-start | bytes 1572872 | tf_op jit(solution)/shard_map/ppermute | solution.py:288
  127.7 13.4 %collective-permute-start.18 = (bf16[2,256,512]{2,1,0:T(8,128)(2,1)S(1)}, bf16[2,256,512]{2,1,0:T(8,128)(2,1)S(1)}, u32[]{:S(2)}, u32[]{:S(2)}) collective-permute-start(bf16[2,256,512]{2,1,0:T(8,128)(2,1)S(1)} %get-tuple-element.71), channel_id=1, source_target_pairs={{0,64},{32,96},{64,128},{96,160},{128,192},{160,224},{192,0},{224,... | collective-permute-start | bytes 1572872 | tf_op jit(solution)/shard_map/ppermute | solution.py:293
  138.7 14.9 %collective-permute-start.20 = (bf16[2,256,512]{2,1,0:T(8,128)(2,1)S(1)}, bf16[2,256,512]{2,1,0:T(8,128)(2,1)S(1)}, u32[]{:S(2)}, u32[]{:S(2)}) collective-permute-start(bf16[2,256,512]{2,1,0:T(8,128)(2,1)S(1)} %local_params.5.a_ref), channel_id=1, source_target_pairs={{0,2},{1,3},{2,0},{3,1},{4,6},{5,7},{6,4},{7,5},{8,10},{9,11},{10,... | collective-permute-start | bytes 1572872 | tf_op jit(solution)/shard_map/ppermute | solution.py:288
  139.8 13.9 %collective-permute-start.17 = (bf16[2,256,512]{2,1,0:T(8,128)(2,1)S(1)}, bf16[2,256,512]{2,1,0:T(8,128)(2,1)S(1)}, u32[]{:S(2)}, u32[]{:S(2)}) collective-permute-start(bf16[2,256,512]{2,1,0:T(8,128)(2,1)S(1)} %get-tuple-element.70), channel_id=1, source_target_pairs={{0,128},{32,160},{64,192},{96,224},{128,0},{160,32},{192,64},{224,... | collective-permute-start | bytes 1572872 | tf_op jit(solution)/shard_map/ppermute | solution.py:293
  141.4 23.5 %collective-permute-start.22 = (bf16[2,256,512]{2,1,0:T(8,128)(2,1)S(1)}, bf16[2,256,512]{2,1,0:T(8,128)(2,1)S(1)}, u32[]{:S(2)}, u32[]{:S(2)}) collective-permute-start(bf16[2,256,512]{2,1,0:T(8,128)(2,1)S(1)} %local_params.6.a_ref), channel_id=1, source_target_pairs={{0,2},{1,3},{2,0},{3,1},{4,6},{5,7},{6,4},{7,5},{8,10},{9,11},{10,... | collective-permute-start | bytes 1572872 | tf_op jit(solution)/shard_map/ppermute | solution.py:288
  154.0 18.8 %collective-permute-start.21 = (bf16[2,256,512]{2,1,0:T(8,128)(2,1)S(1)}, bf16[2,256,512]{2,1,0:T(8,128)(2,1)S(1)}, u32[]{:S(2)}, u32[]{:S(2)}) collective-permute-start(bf16[2,256,512]{2,1,0:T(8,128)(2,1)S(1)} %local_params.7.a_ref), channel_id=1, source_target_pairs={{0,2},{1,3},{2,0},{3,1},{4,6},{5,7},{6,4},{7,5},{8,10},{9,11},{10,... | collective-permute-start | bytes 1572872 | tf_op jit(solution)/shard_map/ppermute | solution.py:288

commit v4 on v3

--- a/solution.py
+++ b/solution.py
@@ -323,14 +323,14 @@
     u_own = update(gram0, after(other0, gram1), rows0)
     u_peer = [flip(u, "replica", 1) for u in u_own]
 
-    w = update(gram1, after(other1, mb_peer, ma_peer), rows1, u_own, u_peer)
+    w = update(gram1, after(other1, ma_peer), rows1, u_own, u_peer)
     back = [w[0], shift(w[1], -1), None, shift(w[3], -3)]
     back[2] = shift(after(w[2], back[1]), -2)
     p_own = [None] * 4
     a_peer = [None] * 4
     p_own[0] = local(y, 0, params, p_peer, back[0])
     a_peer[0] = flip(p_own[0], "replica", 2)
-    p_own[1] = local(y, 1, params, p_peer, after(back[1], p_own[0]))
+    p_own[1] = local(y, 1, params, p_peer, after(back[1], p_own[0], mb_peer))
     a_peer[1] = flip(p_own[1], "replica", 2)
     p_own[3] = local(y, 3, params, p_peer, after(back[3], p_own[1]))
     a_peer[3] = flip(p_own[3], "replica", 2)

time: 174 us -> 168 us (0.966)
  the two profiles are of different devices: /device:TPU:66 before, /device:TPU:2 now
where the time goes in v4:
time: 168 us
  waiting for transfers between devices  92.4 us (55%)
  starting transfers between devices  38.4 us (23%)
  Pallas kernels  32.1 us (19%)
  local copies, waits for them, and re-layouts  3.78 us (2%)
    ppermute x14, waiting for transfers between devices, flip(): lax.ppermute(value, axis, [(s, s ^ mask) for s in range(lax.axis_size(axi...  51.4 us
    ppermute x9, waiting for transfers between devices, shift(): lax.ppermute(value, 'fsdp', [(s, (s + 2 * d) % count) for s in range(coun...  40.9 us
    ppermute x14, starting transfers between devices, flip(): lax.ppermute(value, axis, [(s, s ^ mask) for s in range(lax.axis_size(axi...  23 us
    pallas_call x2, Pallas kernels, update(): pl.pallas_call(functools.partial(update_kernel, last), in_specs=[pl.Block...  16.8 us
    ppermute x9, starting transfers between devices, shift(): lax.ppermute(value, 'fsdp', [(s, (s + 2 * d) % count) for s in range(coun...  15.5 us
    pallas_call x6, Pallas kernels, mean_into(): pl.pallas_call(mean_kernel, grid_spec=pltpu.PrefetchScalarGridSpec(num_sc...  6.91 us
    unnamed x8, local copies, waits for them, and re-layouts  3.78 us
  transfers between devices with their start and end apart: 23, of which 13 were waited for; matrix products, arithmetic and copies ran while one was open for 0% of the time, Pallas kernels for 18%

profile of v4, /device:TPU:2, one launch (start us, length us, event | category | flops | bytes accessed | tf_op | source)
XLA Modules:
  0.0 167.5 jit_solution(10877225586402742514)
XLA Ops:
  0.7 2.2 %copy-done.1 = bf16[2,1,8,256,512]{4,3,2,1,0:T(8,128)(2,1)S(1)} copy-done((bf16[2,1,8,256,512]{4,3,2,1,0:T(8,128)(2,1)S(1)}, bf16[2,1,8,256,512]{4,3,2,1,0:T(8,128)(2,1)}, u32[]{:S(2)}) %copy-start.1) | copy-done | bytes 4194328
  2.8 1.6 copy-done.3
  4.4 1.6 nest_first.1
  6.1 4.1 %collective-permute-done.peer_ref = bf16[8,256,512]{2,1,0:T(8,128)(2,1)S(1)} collective-permute-done((bf16[8,256,512]{2,1,0:T(8,128)(2,1)S(1)}, bf16[8,256,512]{2,1,0:T(8,128)(2,1)S(1)}, u32[]{:S(2)}, u32[]{:S(2)}) %collective-permute-start) | collective-permute-done | bytes 2097184 | tf_op jit(solution)/shard_map/ppermute | solution.py:288
  10.4 1.6 collective-permute-start.2
  12.0 2.9 %collective-permute-start.3 = (bf16[2,256,512]{2,1,0:T(8,128)(2,1)S(1)}, bf16[2,256,512]{2,1,0:T(8,128)(2,1)S(1)}, u32[]{:S(2)}, u32[]{:S(2)}) collective-permute-start(bf16[2,256,512]{2,1,0:T(8,128)(2,1)S(1)} %get-tuple-element.49), channel_id=1, source_target_pairs={{0,128},{32,160},{64,192},{96,224},{128,0},{160,32},{192,64},{224,... | collective-permute-start | bytes 1572872 | tf_op jit(solution)/shard_map/ppermute | solution.py:293
  14.9 1.3 collective-permute-start.4
  16.3 3.1 %nest_second.1 = (bf16[6,256,512]{2,1,0:T(8,128)(2,1)S(1)}, bf16[2,256,512]{2,1,0:T(8,128)(2,1)S(1)}, bf16[2,256,512]{2,1,0:T(8,128)(2,1)S(1)}, bf16[2,256,512]{...) custom-call(s32[1]{0:T(128)} %bitcast.y_ref, ...), custom_call_target="tpu_custom_call" | custom-call | flops 10485760 | bytes 10485760 | tf_op jit(solution)/shard_map/nest_second/pallas_call | solution.py:105
  19.4 2.0 %collective-permute-start.9 = (bf16[6,256,512]{2,1,0:T(8,128)(2,1)S(1)}, bf16[6,256,512]{2,1,0:T(8,128)(2,1)S(1)}, u32[]{:S(2)}, u32[]{:S(2)}) collective-permute-start(bf16[6,256,512]{2,1,0:T(8,128)(2,1)S(1)} %get-tuple-element.51.a_ref), channel_id=1, source_target_pairs={{0,2},{1,3},{2,0},{3,1},{4,6},{5,7},{6,4},{7,5},{8,10},{9,11},{10,... | collective-permute-start | bytes 4718600 | tf_op jit(solution)/shard_map/ppermute | solution.py:288
  21.4 4.5 %collective-permute-done.2.refs_1_.refs_3_ = bf16[2,256,512]{2,1,0:T(8,128)(2,1)S(1)} collective-permute-done((bf16[2,256,512]{2,1,0:T(8,128)(2,1)S(1)}, bf16[2,256,512]{2,1,0:T(8,128)(2,1)S(1)}, u32[]{:S(2)}, u32[]{:S(2)}) %collective-permute-start.2) | collective-permute-done | bytes 524320 | tf_op jit(solution)/shard_map/ppermute | solution.py:293
  25.9 12.4 %collective-permute-done.3.refs_2_.refs_4_ = bf16[2,256,512]{2,1,0:T(8,128)(2,1)S(1)} collective-permute-done((bf16[2,256,512]{2,1,0:T(8,128)(2,1)S(1)}, bf16[2,256,512]{2,1,0:T(8,128)(2,1)S(1)}, u32[]{:S(2)}, u32[]{:S(2)}) %collective-permute-start.3) | collective-permute-done | bytes 524320 | tf_op jit(solution)/shard_map/ppermute | solution.py:293
  38.3 1.2 partial_gram.2.refs_0_
  39.6 1.2 collective-permute-start.5
  40.8 2.4 %collective-permute-start.6 = (bf16[2,256,512]{2,1,0:T(8,128)(2,1)S(1)}, bf16[2,256,512]{2,1,0:T(8,128)(2,1)S(1)}, u32[]{:S(2)}, u32[]{:S(2)}) collective-permute-start(bf16[2,256,512]{2,1,0:T(8,128)(2,1)S(1)} %get-tuple-element.58), channel_id=1, source_target_pairs={{0,128},{32,160},{64,192},{96,224},{128,0},{160,32},{192,64},{224,... | collective-permute-start | bytes 1572872 | tf_op jit(solution)/shard_map/ppermute | solution.py:293
  43.2 1.7 collective-permute-start.7
  44.9 7.2 %collective-permute-start.10 = (bf16[2,528,256]{2,1,0:T(8,128)(2,1)S(1)}, bf16[2,528,256]{2,1,0:T(8,128)(2,1)S(1)}, u32[]{:S(2)}, u32[]{:S(2)}) collective-permute-start(bf16[2,528,256]{2,1,0:T(8,128)(2,1)S(1)} %partial_gram.2.refs_0_), channel_id=1, source_target_pairs={{0,32},{32,0},{64,96},{96,64},{128,160},{160,128},{192,224},{224,1... | collective-permute-start | bytes 1622024 | tf_op jit(solution)/shard_map/ppermute | solution.py:288
  52.1 2.4 %collective-permute-done.5.refs_1_.refs_3_ = bf16[2,256,512]{2,1,0:T(8,128)(2,1)S(1)} collective-permute-done((bf16[2,256,512]{2,1,0:T(8,128)(2,1)S(1)}, bf16[2,256,512]{2,1,0:T(8,128)(2,1)S(1)}, u32[]{:S(2)}, u32[]{:S(2)}) %collective-permute-start.5) | collective-permute-done | bytes 524320 | tf_op jit(solution)/shard_map/ppermute | solution.py:293
  54.4 11.8 %collective-permute-done.6.refs_2_.refs_4_ = bf16[2,256,512]{2,1,0:T(8,128)(2,1)S(1)} collective-permute-done((bf16[2,256,512]{2,1,0:T(8,128)(2,1)S(1)}, bf16[2,256,512]{2,1,0:T(8,128)(2,1)S(1)}, u32[]{:S(2)}, u32[]{:S(2)}) %collective-permute-start.6) | collective-permute-done | bytes 524320 | tf_op jit(solution)/shard_map/ppermute | solution.py:293
  66.2 1.2 partial_gram.3.refs_0_
  67.5 7.5 %collective-permute-start.8 = (bf16[2,528,256]{2,1,0:T(8,128)(2,1)S(1)}, bf16[2,528,256]{2,1,0:T(8,128)(2,1)S(1)}, u32[]{:S(2)}, u32[]{:S(2)}) collective-permute-start(bf16[2,528,256]{2,1,0:T(8,128)(2,1)S(1)} %partial_gram.3.refs_0_), channel_id=1, source_target_pairs={{0,32},{32,0},{64,96},{96,64},{128,160},{160,128},{192,224},{224,1... | collective-permute-start | bytes 1622024 | tf_op jit(solution)/shard_map/ppermute | solution.py:288
  75.0 8.2 %newton_schulz.2 = (bf16[2,256,512]{2,1,0:T(8,128)(2,1)S(1)}, bf16[2,256,512]{2,1,0:T(8,128)(2,1)S(1)}, bf16[2,256,512]{2,1,0:T(8,128)(2,1)S(1)}, bf16[2,256,512]{2,1,0:T(8,128)(2,1)S(1)}) custom-call(bf16[2,528,256]{2,1,0:T(8,128)(2,1)S(1)} %partial_gram.2.refs_0_, bf16[2,528,256]{2,1,0:T(8,128)(2,1)S(1)} %collective-permute-done.10.refs_1_, ...), custom_call_target="tpu_custom_call" | custom-call | flops 6979321856 | bytes 8388608 | tf_op jit(solution)/shard_map/newton_schulz/pallas_call | solution.py:226
  84.3 23.6 %collective-permute-done.8.refs_1_ = bf16[2,528,256]{2,1,0:T(8,128)(2,1)S(1)} collective-permute-done((bf16[2,528,256]{2,1,0:T(8,128)(2,1)S(1)}, bf16[2,528,256]{2,1,0:T(8,128)(2,1)S(1)}, u32[]{:S(2)}, u32[]{:S(2)}) %collective-permute-start.8) | collective-permute-done | bytes 540704 | tf_op jit(solution)/shard_map/ppermute | solution.py:288
  108.0 8.6 %newton_schulz.3 = (bf16[2,256,512]{2,1,0:T(8,128)(2,1)S(1)}, bf16[2,256,512]{2,1,0:T(8,128)(2,1)S(1)}, bf16[2,256,512]{2,1,0:T(8,128)(2,1)S(1)}, bf16[2,256,512]{2,1,0:T(8,128)(2,1)S(1)}) custom-call(bf16[2,528,256]{2,1,0:T(8,128)(2,1)S(1)} %partial_gram.3.refs_0_, bf16[2,528,256]{2,1,0:T(8,128)(2,1)S(1)} %collective-permute-done.8.refs_1_, ...), custom_call_target="tpu_custom_call" | custom-call | flops 6979321856 | bytes 8388608 | tf_op jit(solution)/shard_map/newton_schulz/pallas_call | solution.py:226
  116.6 2.3 %collective-permute-start.15 = (bf16[2,256,512]{2,1,0:T(8,128)(2,1)S(1)}, bf16[2,256,512]{2,1,0:T(8,128)(2,1)S(1)}, u32[]{:S(2)}, u32[]{:S(2)}) collective-permute-start(bf16[2,256,512]{2,1,0:T(8,128)(2,1)S(1)} %get-tuple-element.67), channel_id=1, source_target_pairs={{0,192},{32,224},{64,0},{96,32},{128,64},{160,96},{192,128},{224,1... | collective-permute-start | bytes 1572872 | tf_op jit(solution)/shard_map/ppermute | solution.py:293
  119.4 1.7 %collective-permute-start.17 = (bf16[2,256,512]{2,1,0:T(8,128)(2,1)S(1)}, bf16[2,256,512]{2,1,0:T(8,128)(2,1)S(1)}, u32[]{:S(2)}, u32[]{:S(2)}) collective-permute-start(bf16[2,256,512]{2,1,0:T(8,128)(2,1)S(1)} %get-tuple-element.69), channel_id=1, source_target_pairs={{0,64},{32,96},{64,128},{96,160},{128,192},{160,224},{192,0},{224,... | collective-permute-start | bytes 1572872 | tf_op jit(solution)/shard_map/ppermute | solution.py:293
  122.1 8.4 %collective-permute-done.15.w_ref = bf16[2,256,512]{2,1,0:T(8,128)(2,1)S(1)} collective-permute-done((bf16[2,256,512]{2,1,0:T(8,128)(2,1)S(1)}, bf16[2,256,512]{2,1,0:T(8,128)(2,1)S(1)}, u32[]{:S(2)}, u32[]{:S(2)}) %collective-permute-start.15) | collective-permute-done | bytes 524320 | tf_op jit(solution)/shard_map/ppermute | solution.py:293
  130.7 1.8 %collective-permute-start.20 = (bf16[2,256,512]{2,1,0:T(8,128)(2,1)S(1)}, bf16[2,256,512]{2,1,0:T(8,128)(2,1)S(1)}, u32[]{:S(2)}, u32[]{:S(2)}) collective-permute-start(bf16[2,256,512]{2,1,0:T(8,128)(2,1)S(1)} %local_params.5.a_ref), channel_id=1, source_target_pairs={{0,2},{1,3},{2,0},{3,1},{4,6},{5,7},{6,4},{7,5},{8,10},{9,11},{10,... | collective-permute-start | bytes 1572872 | tf_op jit(solution)/shard_map/ppermute | solution.py:288
  134.1 1.7 %collective-permute-start.22 = (bf16[2,256,512]{2,1,0:T(8,128)(2,1)S(1)}, bf16[2,256,512]{2,1,0:T(8,128)(2,1)S(1)}, u32[]{:S(2)}, u32[]{:S(2)}) collective-permute-start(bf16[2,256,512]{2,1,0:T(8,128)(2,1)S(1)} %local_params.6.a_ref), channel_id=1, source_target_pairs={{0,2},{1,3},{2,0},{3,1},{4,6},{5,7},{6,4},{7,5},{8,10},{9,11},{10,... | collective-permute-start | bytes 1572872 | tf_op jit(solution)/shard_map/ppermute | solution.py:288
  135.8 9.9 %collective-permute-done.20.b_ref = bf16[2,256,512]{2,1,0:T(8,128)(2,1)S(1)} collective-permute-done((bf16[2,256,512]{2,1,0:T(8,128)(2,1)S(1)}, bf16[2,256,512]{2,1,0:T(8,128)(2,1)S(1)}, u32[]{:S(2)}, u32[]{:S(2)}) %collective-permute-start.20) | collective-permute-done | bytes 524320 | tf_op jit(solution)/shard_map/ppermute | solution.py:288
  147.8 2.5 %replica_mean.6.refs_0_ = bf16[8,256,512]{2,1,0:T(8,128)(2,1)} custom-call(s32[1]{0:T(128)} %bitcast.y_ref, bf16[6,256,512]{2,1,0:T(8,128)(2,1)S(1)} %get-tuple-element.51.a_ref, bf16[6,256,512]{2,1,0:T(8,128)(2,1)S(1)} %collective-permute-done.9.b_ref), custom_call_target="tpu_custom_call" | custom-call | flops 1048576 | bytes 2097152 | tf_op jit(solution)/shard_map/replica_mean/pallas_call | solution.py:271
  152.1 4.9 %collective-permute-done.22.b_ref = bf16[2,256,512]{2,1,0:T(8,128)(2,1)S(1)} collective-permute-done((bf16[2,256,512]{2,1,0:T(8,128)(2,1)S(1)}, bf16[2,256,512]{2,1,0:T(8,128)(2,1)S(1)}, u32[]{:S(2)}, u32[]{:S(2)}) %collective-permute-start.22) | collective-permute-done | bytes 524320 | tf_op jit(solution)/shard_map/ppermute | solution.py:288
  158.7 7.9 %collective-permute-done.21.b_ref = bf16[2,256,512]{2,1,0:T(8,128)(2,1)S(1)} collective-permute-done((bf16[2,256,512]{2,1,0:T(8,128)(2,1)S(1)}, bf16[2,256,512]{2,1,0:T(8,128)(2,1)S(1)}, u32[]{:S(2)}, u32[]{:S(2)}) %collective-permute-start.21) | collective-permute-done | bytes 524320 | tf_op jit(solution)/shard_map/ppermute | solution.py:288
  (38 shorter events, 11.3 us)
Async XLA Ops:
  0.6 2.2 %copy-start.1 = (bf16[2,1,8,256,512]{4,3,2,1,0:T(8,128)(2,1)S(1)}, bf16[2,1,8,256,512]{4,3,2,1,0:T(8,128)(2,1)}, u32[]{:S(2)}) copy-start(bf16[2,1,8,256,512]{4,3,2,1,0:T(8,128)(2,1)} %g_ref.3) | copy-start | bytes 12582916
  2.8 1.6 copy-start.3
  4.4 5.9 %copy-start = (bf16[1,8,256,512]{3,2,1,0:T(8,128)(2,1)S(1)}, bf16[1,8,256,512]{3,2,1,0:T(8,128)(2,1)}, u32[]{:S(2)}) copy-start(bf16[1,8,256,512]{3,2,1,0:T(8,128)(2,1)} %param.3) | copy-start | bytes 6291460
  4.4 11.8 %copy-start.2 = (bf16[2,1,8,256,512]{4,3,2,1,0:T(8,128)(2,1)S(1)}, bf16[2,1,8,256,512]{4,3,2,1,0:T(8,128)(2,1)}, u32[]{:S(2)}) copy-start(bf16[2,1,8,256,512]{4,3,2,1,0:T(8,128)(2,1)} %g_ref.3) | copy-start | bytes 12582916
  6.0 4.2 %collective-permute-start = (bf16[8,256,512]{2,1,0:T(8,128)(2,1)S(1)}, bf16[8,256,512]{2,1,0:T(8,128)(2,1)S(1)}, u32[]{:S(2)}, u32[]{:S(2)}) collective-permute-start(bf16[8,256,512]{2,1,0:T(8,128)(2,1)S(1)} %get-tuple-element.41.m_ref), channel_id=1, source_target_pairs={{0,1},{1,0},{2,3},{3,2},{4,5},{5,4},{6,7},{7,6},{8,9},{9,8},{10,11... | collective-permute-start | bytes 6291464 | tf_op jit(solution)/shard_map/ppermute | solution.py:288
  10.3 28.0 %collective-permute-start.1 = (bf16[8,256,512]{2,1,0:T(8,128)(2,1)S(1)}, bf16[8,256,512]{2,1,0:T(8,128)(2,1)S(1)}, u32[]{:S(2)}, u32[]{:S(2)}) collective-permute-start(bf16[8,256,512]{2,1,0:T(8,128)(2,1)S(1)} %bitcast.5), channel_id=1, source_target_pairs={{0,1},{1,0},{2,3},{3,2},{4,5},{5,4},{6,7},{7,6},{8,9},{9,8},{10,11... | collective-permute-start | bytes 6291464 | tf_op jit(solution)/shard_map/ppermute | solution.py:288
  10.4 15.5 %collective-permute-start.2 = (bf16[2,256,512]{2,1,0:T(8,128)(2,1)S(1)}, bf16[2,256,512]{2,1,0:T(8,128)(2,1)S(1)}, u32[]{:S(2)}, u32[]{:S(2)}) collective-permute-start(bf16[2,256,512]{2,1,0:T(8,128)(2,1)S(1)} %get-tuple-element.48), channel_id=1, source_target_pairs={{0,64},{32,96},{64,128},{96,160},{128,192},{160,224},{192,0},{224,... | collective-permute-start | bytes 1572872 | tf_op jit(solution)/shard_map/ppermute | solution.py:293
  12.0 26.3 %collective-permute-start.3 = (bf16[2,256,512]{2,1,0:T(8,128)(2,1)S(1)}, bf16[2,256,512]{2,1,0:T(8,128)(2,1)S(1)}, u32[]{:S(2)}, u32[]{:S(2)}) collective-permute-start(bf16[2,256,512]{2,1,0:T(8,128)(2,1)S(1)} %get-tuple-element.49), channel_id=1, source_target_pairs={{0,128},{32,160},{64,192},{96,224},{128,0},{160,32},{192,64},{224,... | collective-permute-start | bytes 1572872 | tf_op jit(solution)/shard_map/ppermute | solution.py:293
  14.9 23.4 %collective-permute-start.4 = (bf16[2,256,512]{2,1,0:T(8,128)(2,1)S(1)}, bf16[2,256,512]{2,1,0:T(8,128)(2,1)S(1)}, u32[]{:S(2)}, u32[]{:S(2)}) collective-permute-start(bf16[2,256,512]{2,1,0:T(8,128)(2,1)S(1)} %get-tuple-element.50), channel_id=1, source_target_pairs={{0,192},{32,224},{64,0},{96,32},{128,64},{160,96},{192,128},{224,1... | collective-permute-start | bytes 1572872 | tf_op jit(solution)/shard_map/ppermute | solution.py:293
  19.4 64.5 %collective-permute-start.9 = (bf16[6,256,512]{2,1,0:T(8,128)(2,1)S(1)}, bf16[6,256,512]{2,1,0:T(8,128)(2,1)S(1)}, u32[]{:S(2)}, u32[]{:S(2)}) collective-permute-start(bf16[6,256,512]{2,1,0:T(8,128)(2,1)S(1)} %get-tuple-element.51.a_ref), channel_id=1, source_target_pairs={{0,2},{1,3},{2,0},{3,1},{4,6},{5,7},{6,4},{7,5},{8,10},{9,11},{10,... | collective-permute-start | bytes 4718600 | tf_op jit(solution)/shard_map/ppermute | solution.py:288
  39.6 14.8 %collective-permute-start.5 = (bf16[2,256,512]{2,1,0:T(8,128)(2,1)S(1)}, bf16[2,256,512]{2,1,0:T(8,128)(2,1)S(1)}, u32[]{:S(2)}, u32[]{:S(2)}) collective-permute-start(bf16[2,256,512]{2,1,0:T(8,128)(2,1)S(1)} %get-tuple-element.57), channel_id=1, source_target_pairs={{0,64},{32,96},{64,128},{96,160},{128,192},{160,224},{192,0},{224,... | collective-permute-start | bytes 1572872 | tf_op jit(solution)/shard_map/ppermute | solution.py:293
  40.8 25.4 %collective-permute-start.6 = (bf16[2,256,512]{2,1,0:T(8,128)(2,1)S(1)}, bf16[2,256,512]{2,1,0:T(8,128)(2,1)S(1)}, u32[]{:S(2)}, u32[]{:S(2)}) collective-permute-start(bf16[2,256,512]{2,1,0:T(8,128)(2,1)S(1)} %get-tuple-element.58), channel_id=1, source_target_pairs={{0,128},{32,160},{64,192},{96,224},{128,0},{160,32},{192,64},{224,... | collective-permute-start | bytes 1572872 | tf_op jit(solution)/shard_map/ppermute | solution.py:293
  43.2 23.1 %collective-permute-start.7 = (bf16[2,256,512]{2,1,0:T(8,128)(2,1)S(1)}, bf16[2,256,512]{2,1,0:T(8,128)(2,1)S(1)}, u32[]{:S(2)}, u32[]{:S(2)}) collective-permute-start(bf16[2,256,512]{2,1,0:T(8,128)(2,1)S(1)} %get-tuple-element.59), channel_id=1, source_target_pairs={{0,192},{32,224},{64,0},{96,32},{128,64},{160,96},{192,128},{224,1... | collective-permute-start | bytes 1572872 | tf_op jit(solution)/shard_map/ppermute | solution.py:293
  44.9 30.1 %collective-permute-start.10 = (bf16[2,528,256]{2,1,0:T(8,128)(2,1)S(1)}, bf16[2,528,256]{2,1,0:T(8,128)(2,1)S(1)}, u32[]{:S(2)}, u32[]{:S(2)}) collective-permute-start(bf16[2,528,256]{2,1,0:T(8,128)(2,1)S(1)} %partial_gram.2.refs_0_), channel_id=1, source_target_pairs={{0,32},{32,0},{64,96},{96,64},{128,160},{160,128},{192,224},{224,1... | collective-permute-start | bytes 1622024 | tf_op jit(solution)/shard_map/ppermute | solution.py:288
  67.5 40.4 %collective-permute-start.8 = (bf16[2,528,256]{2,1,0:T(8,128)(2,1)S(1)}, bf16[2,528,256]{2,1,0:T(8,128)(2,1)S(1)}, u32[]{:S(2)}, u32[]{:S(2)}) collective-permute-start(bf16[2,528,256]{2,1,0:T(8,128)(2,1)S(1)} %partial_gram.3.refs_0_), channel_id=1, source_target_pairs={{0,32},{32,0},{64,96},{96,64},{128,160},{160,128},{192,224},{224,1... | collective-permute-start | bytes 1622024 | tf_op jit(solution)/shard_map/ppermute | solution.py:288
  83.2 24.8 %collective-permute-start.11 = (bf16[2,256,512]{2,1,0:T(8,128)(2,1)S(1)}, bf16[2,256,512]{2,1,0:T(8,128)(2,1)S(1)}, u32[]{:S(2)}, u32[]{:S(2)}) collective-permute-start(bf16[2,256,512]{2,1,0:T(8,128)(2,1)S(1)} %get-tuple-element.62.refs_6_), channel_id=1, source_target_pairs={{0,1},{1,0},{2,3},{3,2},{4,5},{5,4},{6,7},{7,6},{8,9},{9,8},{10,11... | collective-permute-start | bytes 1572872 | tf_op jit(solution)/shard_map/ppermute | solution.py:288
  83.3 24.7 %collective-permute-start.12 = (bf16[2,256,512]{2,1,0:T(8,128)(2,1)S(1)}, bf16[2,256,512]{2,1,0:T(8,128)(2,1)S(1)}, u32[]{:S(2)}, u32[]{:S(2)}) collective-permute-start(bf16[2,256,512]{2,1,0:T(8,128)(2,1)S(1)} %get-tuple-element.63.refs_7_), channel_id=1, source_target_pairs={{0,1},{1,0},{2,3},{3,2},{4,5},{5,4},{6,7},{7,6},{8,9},{9,8},{10,11... | collective-permute-start | bytes 1572872 | tf_op jit(solution)/shard_map/ppermute | solution.py:288
  83.8 24.2 %collective-permute-start.13 = (bf16[2,256,512]{2,1,0:T(8,128)(2,1)S(1)}, bf16[2,256,512]{2,1,0:T(8,128)(2,1)S(1)}, u32[]{:S(2)}, u32[]{:S(2)}) collective-permute-start(bf16[2,256,512]{2,1,0:T(8,128)(2,1)S(1)} %get-tuple-element.64.refs_8_), channel_id=1, source_target_pairs={{0,1},{1,0},{2,3},{3,2},{4,5},{5,4},{6,7},{7,6},{8,9},{9,8},{10,11... | collective-permute-start | bytes 1572872 | tf_op jit(solution)/shard_map/ppermute | solution.py:288
  83.9 24.1 %collective-permute-start.14 = (bf16[2,256,512]{2,1,0:T(8,128)(2,1)S(1)}, bf16[2,256,512]{2,1,0:T(8,128)(2,1)S(1)}, u32[]{:S(2)}, u32[]{:S(2)}) collective-permute-start(bf16[2,256,512]{2,1,0:T(8,128)(2,1)S(1)} %get-tuple-element.65.refs_9_), channel_id=1, source_target_pairs={{0,1},{1,0},{2,3},{3,2},{4,5},{5,4},{6,7},{7,6},{8,9},{9,8},{10,11... | collective-permute-start | bytes 1572872 | tf_op jit(solution)/shard_map/ppermute | solution.py:288
  107.9 14.1 %collective-permute-start.18 = (bf16[2,256,512]{2,1,0:T(8,128)(2,1)S(1)}, bf16[2,256,512]{2,1,0:T(8,128)(2,1)S(1)}, u32[]{:S(2)}, u32[]{:S(2)}) collective-permute-start(bf16[2,256,512]{2,1,0:T(8,128)(2,1)S(1)} %get-tuple-element.72.a_ref), channel_id=1, source_target_pairs={{0,2},{1,3},{2,0},{3,1},{4,6},{5,7},{6,4},{7,5},{8,10},{9,11},{10,... | collective-permute-start | bytes 1572872 | tf_op jit(solution)/shard_map/ppermute | solution.py:288
  116.6 13.8 %collective-permute-start.15 = (bf16[2,256,512]{2,1,0:T(8,128)(2,1)S(1)}, bf16[2,256,512]{2,1,0:T(8,128)(2,1)S(1)}, u32[]{:S(2)}, u32[]{:S(2)}) collective-permute-start(bf16[2,256,512]{2,1,0:T(8,128)(2,1)S(1)} %get-tuple-element.67), channel_id=1, source_target_pairs={{0,192},{32,224},{64,0},{96,32},{128,64},{160,96},{192,128},{224,1... | collective-permute-start | bytes 1572872 | tf_op jit(solution)/shard_map/ppermute | solution.py:293
  119.2 16.7 %collective-permute-start.19 = (bf16[2,256,512]{2,1,0:T(8,128)(2,1)S(1)}, bf16[2,256,512]{2,1,0:T(8,128)(2,1)S(1)}, u32[]{:S(2)}, u32[]{:S(2)}) collective-permute-start(bf16[2,256,512]{2,1,0:T(8,128)(2,1)S(1)} %local_params.4.a_ref), channel_id=1, source_target_pairs={{0,2},{1,3},{2,0},{3,1},{4,6},{5,7},{6,4},{7,5},{8,10},{9,11},{10,... | collective-permute-start | bytes 1572872 | tf_op jit(solution)/shard_map/ppermute | solution.py:288
  119.4 14.4 %collective-permute-start.17 = (bf16[2,256,512]{2,1,0:T(8,128)(2,1)S(1)}, bf16[2,256,512]{2,1,0:T(8,128)(2,1)S(1)}, u32[]{:S(2)}, u32[]{:S(2)}) collective-permute-start(bf16[2,256,512]{2,1,0:T(8,128)(2,1)S(1)} %get-tuple-element.69), channel_id=1, source_target_pairs={{0,64},{32,96},{64,128},{96,160},{128,192},{160,224},{192,0},{224,... | collective-permute-start | bytes 1572872 | tf_op jit(solution)/shard_map/ppermute | solution.py:293
  130.7 14.9 %collective-permute-start.20 = (bf16[2,256,512]{2,1,0:T(8,128)(2,1)S(1)}, bf16[2,256,512]{2,1,0:T(8,128)(2,1)S(1)}, u32[]{:S(2)}, u32[]{:S(2)}) collective-permute-start(bf16[2,256,512]{2,1,0:T(8,128)(2,1)S(1)} %local_params.5.a_ref), channel_id=1, source_target_pairs={{0,2},{1,3},{2,0},{3,1},{4,6},{5,7},{6,4},{7,5},{8,10},{9,11},{10,... | collective-permute-start | bytes 1572872 | tf_op jit(solution)/shard_map/ppermute | solution.py:288
  132.6 13.8 %collective-permute-start.16 = (bf16[2,256,512]{2,1,0:T(8,128)(2,1)S(1)}, bf16[2,256,512]{2,1,0:T(8,128)(2,1)S(1)}, u32[]{:S(2)}, u32[]{:S(2)}) collective-permute-start(bf16[2,256,512]{2,1,0:T(8,128)(2,1)S(1)} %get-tuple-element.68), channel_id=1, source_target_pairs={{0,128},{32,160},{64,192},{96,224},{128,0},{160,32},{192,64},{224,... | collective-permute-start | bytes 1572872 | tf_op jit(solution)/shard_map/ppermute | solution.py:293
  134.1 22.9 %collective-permute-start.22 = (bf16[2,256,512]{2,1,0:T(8,128)(2,1)S(1)}, bf16[2,256,512]{2,1,0:T(8,128)(2,1)S(1)}, u32[]{:S(2)}, u32[]{:S(2)}) collective-permute-start(bf16[2,256,512]{2,1,0:T(8,128)(2,1)S(1)} %local_params.6.a_ref), channel_id=1, source_target_pairs={{0,2},{1,3},{2,0},{3,1},{4,6},{5,7},{6,4},{7,5},{8,10},{9,11},{10,... | collective-permute-start | bytes 1572872 | tf_op jit(solution)/shard_map/ppermute | solution.py:288
  146.7 20.0 %collective-permute-start.21 = (bf16[2,256,512]{2,1,0:T(8,128)(2,1)S(1)}, bf16[2,256,512]{2,1,0:T(8,128)(2,1)S(1)}, u32[]{:S(2)}, u32[]{:S(2)}) collective-permute-start(bf16[2,256,512]{2,1,0:T(8,128)(2,1)S(1)} %local_params.7.a_ref), channel_id=1, source_target_pairs={{0,2},{1,3},{2,0},{3,1},{4,6},{5,7},{6,4},{7,5},{8,10},{9,11},{10,... | collective-permute-start | bytes 1572872 | tf_op jit(solution)/shard_map/ppermute | solution.py:288
